TPU v7x, 32 devices: a whole 2x2x4 slice. The times are simulated.
32 devices in a mesh: dp: 16 (over z, y, x), tp: 2 (over core).
Axes of the slice: x: 2, y: 2, z: 4, core: 2. Of those that a mesh axis runs over, the one named last changes fastest.
Arguments:
- inputs: bfloat16 [50688, 384], P(('dp', 'tp')), may hold values from -6 to 6
- keep_mask: int32 [50688], P('dp'), may hold values from 0 to 1, as said below
- cotangent: bfloat16 [50688, 384], P(('dp', 'tp')), may hold values from -6 to 6
- qkv_master: float32 [3, 384, 384], P(None, 'dp', 'tp'), may hold values from -0.3125 to 0.3125
- qkv_first: float32 [3, 384, 384], P(None, 'dp', 'tp'), may hold values from -160 to 160
- qkv_second: float32 [3, 384, 384], P(None, 'dp', 'tp'), may hold values from 25.344 to 405.504
- proj_master: float32 [384, 384], P('tp', 'dp'), may hold values from -3.5 to 3.5
- proj_first: float32 [384, 384], P('tp', 'dp'), may hold values from -24 to 24
- proj_second: float32 [384, 384], P('tp', 'dp'), may hold values from 0.57024 to 9.12384
- fc1_master: float32 [384, 1536], P('dp', 'tp'), may hold values from -0.3125 to 0.3125
- fc1_first: float32 [384, 1536], P('dp', 'tp'), may hold values from -64 to 64
- fc1_second: float32 [384, 1536], P('dp', 'tp'), may hold values from 4.05504 to 64.88064
- fc2_master: float32 [1536, 384], P('tp', 'dp'), may hold values from -0.15625 to 0.15625
- fc2_first: float32 [1536, 384], P('tp', 'dp'), may hold values from -112 to 112
- fc2_second: float32 [1536, 384], P('tp', 'dp'), may hold values from 12.41856 to 198.69696
- norm_master: float32 [6, 384], replicated, may hold values from -4 to 4, as said below
- norm_first: float32 [6, 384], replicated, may hold values from -224 to 224
- norm_second: float32 [6, 384], replicated, may hold values from 57.024 to 912.384
- bias_master: float32 [2, 1152], P('tp'), may hold values from -6 to 6
- bias_first: float32 [2, 1152], P('tp'), may hold values from -160 to 160
- bias_second: float32 [2, 1152], P('tp'), may hold values from 25.344 to 405.504
Outputs:
- output: bfloat16 [50688, 384], P(('dp', 'tp'))
- grad_inputs: float32 [50688, 384], P(('dp', 'tp'))
- qkv_first_new: float32 [3, 384, 384], P(None, 'dp', 'tp')
- qkv_second_new: float32 [3, 384, 384], P(None, 'dp', 'tp')
- qkv_master_new: float32 [3, 384, 384], P(None, 'dp', 'tp')
- qkv_copy: bfloat16 [3, 384, 384], P(None, 'dp', 'tp')
- proj_first_new: float32 [384, 384], P('tp', 'dp')
- proj_second_new: float32 [384, 384], P('tp', 'dp')
- proj_master_new: float32 [384, 384], P('tp', 'dp')
- proj_copy: bfloat16 [384, 384], P('tp', 'dp')
- fc1_first_new: float32 [384, 1536], P('dp', 'tp')
- fc1_second_new: float32 [384, 1536], P('dp', 'tp')
- fc1_master_new: float32 [384, 1536], P('dp', 'tp')
- fc1_copy: bfloat16 [384, 1536], P('dp', 'tp')
- fc2_first_new: float32 [1536, 384], P('tp', 'dp')
- fc2_second_new: float32 [1536, 384], P('tp', 'dp')
- fc2_master_new: float32 [1536, 384], P('tp', 'dp')
- fc2_copy: bfloat16 [1536, 384], P('tp', 'dp')
- norm_first_new: float32 [6, 384], replicated
- norm_second_new: float32 [6, 384], replicated
- norm_master_new: float32 [6, 384], replicated
- bias_first_new: float32 [2, 1152], P('tp')
- bias_second_new: float32 [2, 1152], P('tp')
- bias_master_new: float32 [2, 1152], P('tp')
Inputs may be any that keep to these rules, and one draw needn't show every extreme that they name: `keep_mask`: 1 keeps a token, 0 drops it; the first two tokens of each image of 198 (class and distillation) are always kept. `norm_master`: rows 0 and 2 lie between 0.6 and 1.4.
All inputs are finite; a program needn't handle non-finite values.
Results may differ from a plain program's by a relative error of at most 0.012.
The roundings to bfloat16 on the way count: a program that leaves them out, or rounds other values in their place, can miss the bound.
Values may be sent and summed in bfloat16 or wider, within the bound.
A program may use at most 128 MiB of HBM per device.

v0:
```python
from functools import partial

import jax
import jax.numpy as jnp
from jax import lax
from jax.sharding import PartitionSpec as P

HEAD_DIM = 64
PATCHES = 196
STEP = 5


norm_eps = 1e-06
beta_one = 0.9
beta_two = 0.999
adam_eps = 1e-08
matrix_decay = 0.05


def normalize(values_in, gain_row, shift_row):
    row_mean = jnp.mean(values_in, axis=-1, keepdims=True)
    centred = values_in - row_mean
    variance = jnp.mean(centred * centred, axis=-1, keepdims=True)
    return centred * lax.rsqrt(variance + norm_eps) * gain_row + shift_row


def contract_rows(left_side, right_side):
    return lax.dot_general(
        left_side, right_side, (((0,), (0,)), ((), ())), preferred_element_type=jnp.float32
    )


def contract_cols(left_side, right_side):
    return lax.dot_general(
        left_side, right_side, (((1,), (1,)), ((), ())), preferred_element_type=jnp.float32
    )


def adam_step(master, first, second, grad, rate, decay):
    first = beta_one * first + (1.0 - beta_one) * grad
    second = beta_two * second + (1.0 - beta_two) * grad * grad
    first_hat = first / (1.0 - beta_one**STEP)
    second_hat = second / (1.0 - beta_two**STEP)
    master = master - rate * (first_hat / (jnp.sqrt(second_hat) + adam_eps) + decay * master)
    return (first, second, master)


def body(
    inputs,
    keep_mask,
    cotangent,
    qkv_master,
    qkv_first,
    qkv_second,
    proj_master,
    proj_first,
    proj_second,
    fc1_master,
    fc1_first,
    fc1_second,
    fc2_master,
    fc2_first,
    fc2_second,
    norm_master,
    norm_first,
    norm_second,
    bias_master,
    bias_first,
    bias_second,
):
    dp_count = lax.axis_size("dp")
    tp_count = lax.axis_size("tp")
    dp_index = lax.axis_index("dp")
    tp_index = lax.axis_index("tp")
    local_rows = inputs.shape[0]
    seq_len = PATCHES + 2
    scale_dot = HEAD_DIM ** (-0.5)
    qkv_weight, proj_weight, fc1_weight, fc2_weight = (
        lax.all_gather(qkv_master.astype(jnp.bfloat16), "dp", axis=1, tiled=True),
        lax.all_gather(proj_master.astype(jnp.bfloat16), "dp", axis=1, tiled=True),
        lax.all_gather(fc1_master.astype(jnp.bfloat16), "dp", axis=0, tiled=True),
        lax.all_gather(fc2_master.astype(jnp.bfloat16), "dp", axis=1, tiled=True),
    )
    part_width = qkv_weight.shape[2]
    split_bias = bias_master[0]
    query_bias = split_bias[:part_width]
    value_bias = split_bias[part_width : 2 * part_width]
    hidden_bias = split_bias[2 * part_width :]
    whole_input = lax.all_gather(inputs, "tp", axis=0, tiled=True).astype(jnp.float32)
    row_count = whole_input.shape[0]
    images = row_count // seq_len
    local_heads = part_width // HEAD_DIM
    head_shape = (images, seq_len, local_heads, HEAD_DIM)
    kept_rows = keep_mask.astype(jnp.float32)
    local_kept = lax.dynamic_slice_in_dim(kept_rows, tp_index * local_rows, local_rows, 0)
    key_open = keep_mask.reshape(images, 1, 1, seq_len) > 0
    normed1, norm1_back = jax.vjp(normalize, whole_input, norm_master[0], norm_master[1])
    normed1 = normed1.astype(jnp.bfloat16)
    query_rows = (
        jnp.dot(normed1, qkv_weight[0], preferred_element_type=jnp.float32) + query_bias
    ).astype(jnp.bfloat16)
    key_rows = jnp.dot(normed1, qkv_weight[1], preferred_element_type=jnp.float32).astype(
        jnp.bfloat16
    )
    value_rows = (
        jnp.dot(normed1, qkv_weight[2], preferred_element_type=jnp.float32) + value_bias
    ).astype(jnp.bfloat16)
    query_heads = query_rows.reshape(head_shape)
    key_heads = key_rows.reshape(head_shape)
    value_heads = value_rows.reshape(head_shape)

    def scores_of():
        raw_scores = (
            jnp.einsum(
                "ithd,ishd->ihts", query_heads, key_heads, preferred_element_type=jnp.float32
            )
            * scale_dot
        )
        return jnp.where(key_open, raw_scores, -1000000000.0)

    scores = scores_of()
    top_score = jnp.max(scores, axis=-1, keepdims=True)
    exp_scores = jnp.exp(scores - top_score)
    exp_total = jnp.sum(exp_scores, axis=-1, keepdims=True)
    probs_full = exp_scores / exp_total
    log_total = top_score + jnp.log(exp_total)
    attended = jnp.einsum(
        "ihts,ishd->ithd",
        probs_full.astype(jnp.bfloat16),
        value_heads,
        preferred_element_type=jnp.float32,
    )
    attended = attended.reshape(row_count, part_width).astype(jnp.bfloat16)
    attn_term = jnp.dot(attended, proj_weight, preferred_element_type=jnp.float32)
    attn_full = lax.psum(attn_term, "tp")
    mid_stream = whole_input + (attn_full + norm_master[4])
    normed2, norm2_back = jax.vjp(normalize, mid_stream, norm_master[2], norm_master[3])
    normed2 = normed2.astype(jnp.bfloat16)
    mid_share = lax.dynamic_slice_in_dim(mid_stream, tp_index * local_rows, local_rows, 0)
    pre_act = jnp.dot(normed2, fc1_weight, preferred_element_type=jnp.float32) + hidden_bias
    activated, gelu_back = jax.vjp(partial(jax.nn.gelu, approximate=False), pre_act)
    activated = activated.astype(jnp.bfloat16)
    mlp_share = lax.psum_scatter(
        jnp.dot(activated, fc2_weight, preferred_element_type=jnp.float32).astype(jnp.bfloat16),
        "tp",
        scatter_dimension=0,
        tiled=True,
    ).astype(jnp.float32)
    output = (mid_share + (mlp_share + norm_master[5])).astype(jnp.bfloat16)
    masked = (cotangent.astype(jnp.float32) * local_kept[:, None]).astype(jnp.bfloat16)
    back_whole = lax.all_gather(masked, "tp", axis=0, tiled=True)
    grad_fc2 = contract_rows(activated, back_whole)
    grad_activated = contract_cols(back_whole, fc2_weight)
    grad_pre = gelu_back(grad_activated)[0].astype(jnp.bfloat16)
    grad_fc1 = contract_rows(normed2, grad_pre)
    grad_hidden_bias = jnp.sum(grad_pre.astype(jnp.float32), axis=0)
    norm2_term = contract_cols(grad_pre, fc1_weight)
    back_float = back_whole.astype(jnp.float32)
    grad_out_bias = jnp.sum(back_float, axis=0)
    grad_normed2 = lax.psum(norm2_term, "tp")
    grad_mid, grad_gain2, grad_shift2 = norm2_back(grad_normed2)
    grad_mid = grad_mid + back_float
    grad_branch = grad_mid.astype(jnp.bfloat16)
    grad_proj_bias = jnp.sum(grad_branch.astype(jnp.float32), axis=0)
    grad_mid_share = lax.dynamic_slice_in_dim(grad_mid, tp_index * local_rows, local_rows, 0)
    grad_proj = contract_rows(attended, grad_branch)
    grad_attended = contract_cols(grad_branch, proj_weight).astype(jnp.bfloat16).reshape(head_shape)
    probs_again = jnp.exp(scores_of() - log_total)
    grad_values = jnp.einsum(
        "ihts,ithd->ishd",
        probs_again.astype(jnp.bfloat16),
        grad_attended,
        preferred_element_type=jnp.float32,
    ).astype(jnp.bfloat16)
    grad_probs = jnp.einsum(
        "ithd,ishd->ihts", grad_attended, value_heads, preferred_element_type=jnp.float32
    )
    inner_sum = jnp.sum(probs_again * grad_probs, axis=-1, keepdims=True)
    grad_scores = (probs_again * (grad_probs - inner_sum)).astype(jnp.bfloat16)
    grad_queries = (
        jnp.einsum("ihts,ishd->ithd", grad_scores, key_heads, preferred_element_type=jnp.float32)
        * scale_dot
    ).astype(jnp.bfloat16)
    grad_keys = (
        jnp.einsum("ihts,ithd->ishd", grad_scores, query_heads, preferred_element_type=jnp.float32)
        * scale_dot
    ).astype(jnp.bfloat16)
    grad_stack = jnp.stack(
        [
            grad_queries.reshape(row_count, part_width),
            grad_keys.reshape(row_count, part_width),
            grad_values.reshape(row_count, part_width),
        ]
    )
    grad_qkv = jnp.einsum("rd,crj->cdj", normed1, grad_stack, preferred_element_type=jnp.float32)
    grad_query_bias = jnp.sum(grad_stack[0].astype(jnp.float32), axis=0)
    grad_value_bias = jnp.sum(grad_stack[2].astype(jnp.float32), axis=0)
    norm1_term = jnp.einsum(
        "crj,cdj->rd", grad_stack, qkv_weight, preferred_element_type=jnp.float32
    )
    grad_normed1 = lax.psum(norm1_term, "tp")
    grad_whole, grad_gain1, grad_shift1 = norm1_back(grad_normed1)
    grad_share = (
        lax.dynamic_slice_in_dim(grad_whole, tp_index * local_rows, local_rows, 0) + grad_mid_share
    )
    vector_weight = 0.5
    vector_grad = (
        jnp.stack([grad_gain1, grad_shift1, grad_gain2, grad_shift2, grad_proj_bias, grad_out_bias])
        * vector_weight
    )
    bias_row = jnp.concatenate([grad_query_bias, grad_value_bias, grad_hidden_bias])
    own_row = jnp.arange(tp_count, dtype=jnp.int32)[:, None] == tp_index
    bias_grid = jnp.where(own_row, bias_row[None, :], 0.0)
    vector_sum, bias_total, kept_total = lax.psum(
        (vector_grad, bias_grid, jnp.sum(local_kept)), ("dp", "tp")
    )
    bias_sum = lax.dynamic_slice_in_dim(bias_total, tp_index, 1, 0)
    matrix_grads = (grad_qkv, grad_proj, grad_fc1, grad_fc2)
    summed = lax.psum((matrix_grads[0], matrix_grads[1], matrix_grads[2], matrix_grads[3]), "dp")
    shares = tuple(
        (
            lax.dynamic_slice_in_dim(
                summed_grad,
                dp_index * old_master.shape[split_dim],
                old_master.shape[split_dim],
                split_dim,
            )
            for summed_grad, old_master, split_dim in zip(
                summed, (qkv_master, proj_master, fc1_master, fc2_master), (1, 1, 0, 1)
            )
        )
    )
    grad_scale = row_count * dp_count / kept_total
    outputs = [output, grad_scale * grad_share]
    states = [
        (qkv_master, qkv_first, qkv_second, shares[0], 0.08, matrix_decay, True),
        (proj_master, proj_first, proj_second, shares[1], 0.8, matrix_decay, True),
        (fc1_master, fc1_first, fc1_second, shares[2], 0.08, matrix_decay, True),
        (fc2_master, fc2_first, fc2_second, shares[3], 0.04, matrix_decay, True),
        (norm_master, norm_first, norm_second, vector_sum, 0.5, 0.0, False),
        (bias_master, bias_first, bias_second, bias_sum, 0.5, 0.0, False),
    ]
    for old_master, old_first, old_second, summed_grad, rate, decay, with_copy in states:
        new_first, new_second, new_master = adam_step(
            old_master, old_first, old_second, grad_scale * summed_grad, rate, decay
        )
        outputs.extend([new_first, new_second, new_master])
        if with_copy:
            outputs.append(new_master.astype(jnp.bfloat16))
    return tuple(outputs)


def solution(mesh):
    in_specs = (
        P(("dp", "tp"), None),
        P("dp"),
        P(("dp", "tp"), None),
        P(None, "dp", "tp"),
        P(None, "dp", "tp"),
        P(None, "dp", "tp"),
        P("tp", "dp"),
        P("tp", "dp"),
        P("tp", "dp"),
        P("dp", "tp"),
        P("dp", "tp"),
        P("dp", "tp"),
        P("tp", "dp"),
        P("tp", "dp"),
        P("tp", "dp"),
        P(),
        P(),
        P(),
        P("tp", None),
        P("tp", None),
        P("tp", None),
    )
    out_specs = (
        P(("dp", "tp"), None),
        P(("dp", "tp"), None),
        P(None, "dp", "tp"),
        P(None, "dp", "tp"),
        P(None, "dp", "tp"),
        P(None, "dp", "tp"),
        P("tp", "dp"),
        P("tp", "dp"),
        P("tp", "dp"),
        P("tp", "dp"),
        P("dp", "tp"),
        P("dp", "tp"),
        P("dp", "tp"),
        P("dp", "tp"),
        P("tp", "dp"),
        P("tp", "dp"),
        P("tp", "dp"),
        P("tp", "dp"),
        P(),
        P(),
        P(),
        P("tp", None),
        P("tp", None),
        P("tp", None),
    )
    return jax.shard_map(body, mesh=mesh, in_specs=in_specs, out_specs=out_specs, check_vma=False)
```

profile of v0, /device:TPU:0, one launch (start us, length us, event | category | flops | bytes accessed | tf_op | source)
XLA Modules:
  0.0 609.0 jit_solution(694118227525320632)
XLA Ops:
  10.4 43.4 %all_gather.20 = bf16[192,384]{0,1:T(8,128)(2,1)S(1)} all-gather(bf16[192,24]{0,1:T(8,128)(2,1)S(1)} %convert_element_type.135), channel_id=1, replica_groups=mesh['dp'=16,'tp'=2] {'dp'}, dimensions={1}, use_global_device_ids=true | all-gather | bytes 156672 | tf_op jit(solution)/shard_map/all_gather | solution.py:80
  55.4 38.7 %all_gather.19 = bf16[3,384,192]{2,1,0:T(8,128)(2,1)S(1)} all-gather(bf16[3,24,192]{2,1,0:T(8,128)(2,1)S(1)} %convert_element_type.127), channel_id=1, replica_groups=mesh['dp'=16,'tp'=2] {'dp'}, dimensions={1}, use_global_device_ids=true | all-gather | bytes 470016 | tf_op jit(solution)/shard_map/all_gather | solution.py:79
  107.0 6.7 %reshape.167 = bf16[16,198,3,64]{1,0,3,2:T(8,128)(2,1)} reshape(bf16[3168,192]{0,1:T(8,128)(2,1)} %fusion.15) | data formatting | bytes 2433024 | tf_op jit(solution)/shard_map/reshape | solution.py:108
  117.4 6.7 %reshape.166 = bf16[16,198,3,64]{1,0,3,2:T(8,128)(2,1)} reshape(bf16[3168,192]{0,1:T(8,128)(2,1)} %fusion.14) | data formatting | bytes 2433024 | tf_op jit(solution)/shard_map/reshape | solution.py:110
  124.1 6.7 %reshape.168 = bf16[16,198,3,64]{1,0,3,2:T(8,128)(2,1)} reshape(bf16[3168,192]{0,1:T(8,128)(2,1)} %convolution_convert_fusion.2) | data formatting | bytes 2433024 | tf_op jit(solution)/shard_map/reshape | solution.py:109
  130.8 4.7 fusion.25
  149.7 4.6 fusion.86
  158.3 41.2 %all_gather.22 = bf16[768,384]{0,1:T(8,128)(2,1)S(1)} all-gather(bf16[768,24]{0,1:T(8,128)(2,1)S(1)} %convert_element_type.139), channel_id=1, replica_groups=mesh['dp'=16,'tp'=2] {'dp'}, dimensions={1}, use_global_device_ids=true | all-gather | bytes 626688 | tf_op jit(solution)/shard_map/all_gather | solution.py:82
  199.5 41.7 %all_gather.21 = bf16[384,768]{1,0:T(8,128)(2,1)} all-gather(bf16[24,768]{1,0:T(8,128)(2,1)S(1)} %convert_element_type.137), channel_id=1, replica_groups=mesh['dp'=16,'tp'=2] {'dp'}, dimensions={0}, use_global_device_ids=true | all-gather | bytes 626688 | tf_op jit(solution)/shard_map/all_gather | solution.py:81
  246.5 26.4 %multiply_convert_fusion.1 = (bf16[3168,768]{1,0:T(8,128)(2,1)}, f32[3168,768]{1,0:T(8,128)}, f32[3168,768]{1,0:T(8,128)}) fusion(f32[768]{0:T(1024)S(1)} %slice_reduce_fusion, bf16[384,768]{1,0:T(8,128)(2,1)S(1)} %copy-done.20, f32[3168,384]{1,0:T(8,128)S(1)} %get-tuple-element.124, f32[384]{0:T(512)S(1)} %get-tuple-element.79, ...), kind=kOutput, calls=%fused_computation.10 | convolution fusion | flops 2035224576 | bytes 29817600 | tf_op jit(solution)/shard_map/dot_general | solution.py:140
  272.9 11.4 %convert_reduce_fusion = (f32[768]{0:T(1024)S(1)}, bf16[3168,768]{1,0:T(8,128)(2,1)S(1)}) fusion(f32[3168,768]{1,0:T(8,128)} %get-tuple-element.122, bf16[3168,384]{1,0:T(8,128)(2,1)} %all-gather.5.cloned.1.call-done, bf16[768,384]{0,1:T(8,128)(2,1)S(1)} %all_gather.22, f32[3168,768]{1,0:T(8,128)} %get-tuple-element.130, f32[768]{0:T(1024)S(1)} %slice_reduce_fusion), kind=kOutput, calls=%fused_computation.8 | convolution fusion | flops 1909923072 | bytes 27359232 | tf_op jit(solution)/shard_map/dot_general | solution.py:34
  291.0 6.6 %convolution_convert_fusion = bf16[3168,384]{1,0:T(8,128)(2,1)} fusion(bf16[3168,768]{1,0:T(8,128)(2,1)} %get-tuple-element.121, bf16[768,384]{0,1:T(8,128)(2,1)S(1)} %all_gather.22), kind=kOutput, calls=%fused_computation.38 | convolution fusion | flops 1869778944 | bytes 7888896 | tf_op jit(solution)/shard_map/dot_general | solution.py:144
  297.7 19.7 %all-reduce.9.cloned.1.call-done = f32[3168,384]{1,0:T(8,128)} async-done(((f32[3168,384]{1,0:T(8,128)}), f32[3168,384]{1,0:T(8,128)}) %all-reduce.9.cloned.1.call-update) | async-done | bytes 4866064 | tf_op jit(solution)/shard_map/psum | solution.py:160
  317.4 5.7 multiply_reduce_fusion.1
  323.2 5.7 fusion.82
  333.7 4.8 reshape.169
  339.6 5.9 convert_reduce_fusion.4
  352.1 9.1 %multiply_reduce_fusion = (f32[16,3,198]{2,1,0:T(4,128)S(1)}, f32[16,3,198,198]{2,3,1,0:T(8,128)S(1)}) fusion(f32[16,3,198]{2,1,0:T(4,128)S(1)} %log_add_fusion, f32[16,3,198,198]{2,3,1,0:T(8,128)} %copy-done.1, pred[16,198]{1,0:T(8,128)(4,1)S(1)} %gt.16, bf16[16,198,3,64]{1,0,3,2:T(8,128)(2,1)S(1)} %copy-done.12, bf16[16,198,3,64]{1,0,3,2:T(8,128)(2,1)} %copy-done.13), kind=kOutput, calls=%fused_computation.2 | convolution fusion | flops 250268832 | bytes 17566560 | tf_op jit(solution)/shard_map/ithd,ishd->ihts/dot_general | solution.py:175
  385.7 5.0 convolution_bitcast_fusion
  392.4 5.8 fusion.88
  398.1 9.2 %fusion.68 = f32[384,768]{1,0:T(8,128)} fusion(bf16[3168,768]{1,0:T(8,128)(2,1)} %copy-done.54, f32[3168,384]{1,0:T(8,128)} %copy-done, f32[384]{0:T(512)S(1)} %get-tuple-element.79, f32[384]{0:T(512)S(1)} %get-tuple-element.80, f32[3168]{0:T(1024)S(1)} %fusion.58, f32[3168]{0:T(1024)S(1)} %broadcast_multiply_fusion), kind=kOutput, calls=%fused_computation.154 | convolution fusion | flops 1874644992 | bytes 10940160 | tf_op jit(solution)/shard_map/dot_general | solution.py:28
  425.7 45.0 %all-reduce = (f32[]{:T(128)}, f32[6,384]{1,0:T(8,128)S(1)}, f32[2,1152]{1,0:T(2,128)S(1)}) all-reduce(f32[]{:T(128)} %get-tuple-element.115, f32[6,384]{1,0:T(8,128)S(1)} %broadcast_multiply_fusion.2, f32[2,1152]{1,0:T(2,128)S(1)} %broadcast_select_fusion), channel_id=1, replica_groups=mesh['dp'=16,'tp'=2] {'dp','tp'}, use_global_device_ids=true, to_apply=%region_9.10 | all-reduce | flops 4609 | bytes 36872 | tf_op jit(solution)/shard_map/psum | solution.py:214
  470.8 7.5 %fusion.81 = (f32[3168]{0:T(1024)S(1)}, f32[3168,384]{1,0:T(8,128)}) fusion(f32[3168]{0:T(1024)S(1)} %multiply_multiply_fusion.10, f32[3168]{0:T(1024)S(1)} %copy-done.22, bf16[3168,384]{1,0:T(8,128)(2,1)S(1)} %copy-done.3, f32[3168]{0:T(1024)S(1)} %copy-done.31, f32[3168,384]{1,0:T(8,128)} %all-reduce.11.cloned.1.call-done, f32[384]{0:T(512)S(1)} %copy-done.44), kind=kLoop, calls=%fused_computation.161 | loop fusion | flops 9728928 | bytes 12217344 | tf_op jit(solution)/shard_map/transpose(jvp())/reduce_sum | solution.py:22
  483.5 110.6 %all-reduce.13.cloned.1.call-done = (f32[3,384,192]{2,1,0:T(8,128)}, f32[192,384]{0,1:T(8,128)}, f32[384,768]{1,0:T(8,128)}, f32[768,384]{0,1:T(8,128)}) async-done(((f32[3,384,192]{2,1,0:T(8,128)}, f32[192,384]{0,1:T(8,128)}, f32[384,768]{1,0:T(8,128)}, f32[768,384]{0,1:T(8,128)}), (f32[3,384,192]{2,1,0:T(8,128)}, f32[192,384]{0,1:T(8,128)}, f32[384,768]{1,0:T(8,128)}, ...) | async-done | bytes 3538960 | tf_op jit(solution)/shard_map/psum | solution.py:219
  (213 shorter events, 120.3 us)
Async XLA Ops:
  7.2 87.7 %all-gather.3.cloned.1.call-start = ((), (), s32[]{:S(2)}) async-start(), calls=%async_computation.1 | async-start | bytes 3649536 | tf_op jit(solution)/shard_map/all_gather | solution.py:89
  7.9 233.3 %all-reduce.7.cloned.1.call-start = ((), (), s32[]{:S(2)}) async-start(), calls=%async_computation.2 | async-start | bytes 9732096 | tf_op jit(solution)/shard_map/psum | solution.py:135
  154.2 118.7 %all-gather.5.cloned.1.call-start = ((), (), s32[]{:S(2)}) async-start(), calls=%async_computation.4 | async-start | bytes 3649536 | tf_op jit(solution)/shard_map/all_gather | solution.py:151
  158.2 159.2 %all-reduce.9.cloned.1.call-start = ((), (), s32[]{:S(2)}) async-start(), calls=%async_computation.5 | async-start | bytes 9732096 | tf_op jit(solution)/shard_map/psum | solution.py:160
  290.9 123.1 %reduce-scatter.2.cloned.1.call-start = ((), (), s32[]{:S(2)}) async-start(), calls=%async_computation.3 | async-start | bytes 3649536 | tf_op jit(solution)/shard_map/reduce_scatter | solution.py:143
  297.7 123.7 %all-reduce.11.cloned.1.call-start = ((), (), s32[]{:S(2)}) async-start(), calls=%async_computation.6 | async-start | bytes 9732096 | tf_op jit(solution)/shard_map/psum | solution.py:201
  390.7 203.4 %all-reduce.13.cloned.1.call-start = ((), (), s32[]{:S(2)}) async-start(), calls=%async_computation.7 | async-start | bytes 7864320 | tf_op jit(solution)/shard_map/psum | solution.py:219
  478.2 115.9 %copy-start.35 = (f32[3,24,192]{2,1,0:T(8,128)S(1)}, f32[3,24,192]{2,1,0:T(8,128)}, u32[]{:S(2)}) copy-start(f32[3,24,192]{2,1,0:T(8,128)} %param.26) | copy-start | bytes 165892
  478.2 115.9 %copy-start.36 = (f32[3,24,192]{2,1,0:T(8,128)S(1)}, f32[3,24,192]{2,1,0:T(8,128)}, u32[]{:S(2)}) copy-start(f32[3,24,192]{2,1,0:T(8,128)} %param.25) | copy-start | bytes 165892
  478.2 117.5 %copy-start.27 = (f32[24,768]{1,0:T(8,128)S(1)}, f32[24,768]{1,0:T(8,128)}, u32[]{:S(2)}) copy-start(f32[24,768]{1,0:T(8,128)} %param.30) | copy-start | bytes 221188
  478.2 117.5 %copy-start.37 = (f32[24,768]{1,0:T(8,128)S(1)}, f32[24,768]{1,0:T(8,128)}, u32[]{:S(2)}) copy-start(f32[24,768]{1,0:T(8,128)} %param.32) | copy-start | bytes 221188
  478.2 117.5 %copy-start.38 = (f32[24,768]{1,0:T(8,128)S(1)}, f32[24,768]{1,0:T(8,128)}, u32[]{:S(2)}) copy-start(f32[24,768]{1,0:T(8,128)} %param.31) | copy-start | bytes 221188
  478.3 119.1 %copy-start.29 = (f32[768,24]{0,1:T(8,128)S(1)}, f32[768,24]{0,1:T(8,128)}, u32[]{:S(2)}) copy-start(f32[768,24]{0,1:T(8,128)} %param.33) | copy-start | bytes 221188
  478.3 119.1 %copy-start.39 = (f32[768,24]{0,1:T(8,128)S(1)}, f32[768,24]{0,1:T(8,128)}, u32[]{:S(2)}) copy-start(f32[768,24]{0,1:T(8,128)} %param.35) | copy-start | bytes 221188
  478.3 119.1 %copy-start.40 = (f32[768,24]{0,1:T(8,128)S(1)}, f32[768,24]{0,1:T(8,128)}, u32[]{:S(2)}) copy-start(f32[768,24]{0,1:T(8,128)} %param.34) | copy-start | bytes 221188
  478.3 120.7 %copy-start.34 = (f32[192,24]{0,1:T(8,128)S(1)}, f32[192,24]{0,1:T(8,128)}, u32[]{:S(2)}) copy-start(f32[192,24]{0,1:T(8,128)} %param.27) | copy-start | bytes 55300
  478.3 120.7 %copy-start.45 = (f32[192,24]{0,1:T(8,128)S(1)}, f32[192,24]{0,1:T(8,128)}, u32[]{:S(2)}) copy-start(f32[192,24]{0,1:T(8,128)} %param.29) | copy-start | bytes 55300
  478.3 120.6 %copy-start.46 = (f32[192,24]{0,1:T(8,128)S(1)}, f32[192,24]{0,1:T(8,128)}, u32[]{:S(2)}) copy-start(f32[192,24]{0,1:T(8,128)} %param.28) | copy-start | bytes 55300
  478.3 122.0 %copy-start.41 = (f32[6,384]{1,0:T(8,128)S(1)}, f32[6,384]{1,0:T(8,128)}, u32[]{:S(2)}) copy-start(f32[6,384]{1,0:T(8,128)} %param.36) | copy-start | bytes 27652
  478.3 122.0 %copy-start.49 = (f32[6,384]{1,0:T(8,128)S(1)}, f32[6,384]{1,0:T(8,128)}, u32[]{:S(2)}) copy-start(f32[6,384]{1,0:T(8,128)} %param.38) | copy-start | bytes 27652
  478.4 122.0 %copy-start.50 = (f32[6,384]{1,0:T(8,128)S(1)}, f32[6,384]{1,0:T(8,128)}, u32[]{:S(2)}) copy-start(f32[6,384]{1,0:T(8,128)} %param.37) | copy-start | bytes 27652
  478.4 122.6 %copy-start.48 = (f32[1,1152]{1,0:T(1,128)S(1)}, f32[1,1152]{1,0:T(1,128)}, u32[]{:S(2)}) copy-start(f32[1,1152]{1,0:T(1,128)} %param.39) | copy-start | bytes 13828
  478.4 122.6 %copy-start.52 = (f32[1,1152]{1,0:T(1,128)S(1)}, f32[1,1152]{1,0:T(1,128)}, u32[]{:S(2)}) copy-start(f32[1,1152]{1,0:T(1,128)} %param.41) | copy-start | bytes 13828
  478.4 122.6 %copy-start.53 = (f32[1,1152]{1,0:T(1,128)S(1)}, f32[1,1152]{1,0:T(1,128)}, u32[]{:S(2)}) copy-start(f32[1,1152]{1,0:T(1,128)} %param.40) | copy-start | bytes 13828
  (43 other events, 436.6 us)
Sparse Core Ops, SparseCore 0:
  9.6 13.7 all-gather.2
  154.4 27.2 all-reduce.6
  183.8 12.2 all-gather.4
  291.0 26.3 all-reduce.8
  319.5 11.1 reduce-scatter.1
  390.8 30.5 all-reduce.10
  427.6 166.4 all-reduce.12
where the time goes:
time: 613 us; the launch traced here: 609 us
  blocking collectives  210 us (34%)
  waiting for transfers between devices  134 us (22%)
  matrix products  117 us (19%)
  local copies, waits for them, and re-layouts  66.8 us (11%)
  other arithmetic  64.5 us (11%)
  between operations  16.2 us (3%)
    psum x1, waiting for transfers between devices, body(): lax.psum((matrix_grads[0], matrix_grads[1], matrix_grads[2], matrix_grads...  111 us
    psum x1, blocking collectives, body(): lax.psum((vector_grad, bias_grid, jnp.sum(local_kept)), ('dp', 'tp'))  45 us
    all_gather x1, blocking collectives, body(): lax.all_gather(proj_master.astype(jnp.bfloat16), 'dp', axis=1, tiled=True)  43.4 us
    all_gather x1, blocking collectives, body(): lax.all_gather(fc1_master.astype(jnp.bfloat16), 'dp', axis=0, tiled=True)  41.7 us
    all_gather x1, blocking collectives, body(): lax.all_gather(fc2_master.astype(jnp.bfloat16), 'dp', axis=1, tiled=True)  41.2 us
    all_gather x1, blocking collectives, body(): lax.all_gather(qkv_master.astype(jnp.bfloat16), 'dp', axis=1, tiled=True)  38.7 us
    dot_general x1, matrix products, body(): jnp.dot(normed2, fc1_weight, preferred_element_type=jnp.float32)  26.4 us
    psum x1, waiting for transfers between devices, body(): grad_normed2 = lax.psum(norm2_term, 'tp')  19.7 us
  transfers between devices with their start and end apart: 7, of which 3 were waited for; matrix products, arithmetic and copies ran while one was open for 25% of the time, Pallas kernels for 0%

commit v1 on v0

v1 whole, which is shorter than its diff:
```python
import functools

import jax
import jax.numpy as jnp
from jax import lax
from jax.experimental import pallas as pl
from jax.experimental.pallas import tpu as pltpu
from jax.sharding import PartitionSpec as P

HEAD_DIM = 64
PATCHES = 196
STEP = 5

norm_eps = 1e-06
beta_one = 0.9
beta_two = 0.999
adam_eps = 1e-08
matrix_decay = 0.05

F32 = jnp.float32
BF16 = jnp.bfloat16
MESH = pl.DeviceIdType.MESH
SEQ = PATCHES + 2
PAD = 208
NEG = -1000000000.0
SCALE = HEAD_DIM**-0.5


def dot_nn(a, b):
    return lax.dot_general(a, b, (((1,), (0,)), ((), ())), preferred_element_type=F32)


def dot_nt(a, b):
    return lax.dot_general(a, b, (((1,), (1,)), ((), ())), preferred_element_type=F32)


def dot_tn(a, b):
    return lax.dot_general(a, b, (((0,), (0,)), ((), ())), preferred_element_type=F32)


def norm_parts(v):
    mean = jnp.mean(v, axis=-1, keepdims=True)
    centred = v - mean
    var = jnp.mean(centred * centred, axis=-1, keepdims=True)
    rstd = lax.rsqrt(var + norm_eps)
    return centred * rstd, rstd


def norm_back(grad, xhat, rstd, gain):
    u = grad * gain
    return (
        u
        - jnp.mean(u, axis=-1, keepdims=True)
        - xhat * jnp.mean(u * xhat, axis=-1, keepdims=True)
    ) * rstd


def gelu_parts(u):
    gauss = jnp.exp(-0.5 * u * u)
    t = 1.0 / (1.0 + (0.3275911 * 0.7071067811865476) * jnp.abs(u))
    poly = t * (
        0.5 * 0.254829592
        + t
        * (
            0.5 * -0.284496736
            + t * (0.5 * 1.421413741 + t * (0.5 * -1.453152027 + t * (0.5 * 1.061405429)))
        )
    )
    tail = poly * gauss
    cdf = jnp.where(u < 0.0, tail, 1.0 - tail)
    return u * cdf, cdf + u * (0.3989422804014327 * gauss)


def adam(master, first, second, grad, rate, decay):
    first = beta_one * first + (1.0 - beta_one) * grad
    second = beta_two * second + (1.0 - beta_two) * grad * grad
    first_hat = first / (1.0 - beta_one**STEP)
    second_hat = second / (1.0 - beta_two**STEP)
    master = master - rate * (first_hat / (jnp.sqrt(second_hat) + adam_eps) + decay * master)
    return first, second, master


def kernel(
    nl,
    np_,
    x_h,
    keep_v,
    cot_h,
    qm,
    qf,
    qs,
    pm,
    pf,
    ps,
    am,
    af,
    as_,
    cm,
    cf,
    cs,
    nm,
    nf,
    ns,
    bm,
    bf,
    bs,
    out_h,
    gin_h,
    qf_o,
    qs_o,
    qm_o,
    qc_o,
    pf_o,
    ps_o,
    pm_o,
    pc_o,
    af_o,
    as_o,
    am_o,
    ac_o,
    cf_o,
    cs_o,
    cm_o,
    cc_o,
    nf_o,
    ns_o,
    nm_o,
    bf_o,
    bs_o,
    bm_o,
    wbuf,
    wts,
    grd,
    sib,
    rpl,
    lsn,
    rln,
    fin,
    pk,
    tr_a,
    tr_b,
    bias2,
    cntl,
    cntp,
    vec,
    vsib,
    vpl,
    vln,
    stage,
    mid,
    probs,
    mcol,
    mkt,
    xpad,
    back,
    n1,
    qkv,
    att,
    n2,
    gbr,
    gatt,
    opad,
    act,
    gp,
    dma_sem,
    bar_sems,
    ag_ls,
    ag_lr,
    ag_ps,
    ag_pr,
    ag_ss,
    ag_sr,
    rs_ss,
    rs_sr,
    rs_ps,
    rs_pr,
    rs_ls,
    rs_lr,
    cn_s,
    cn_r,
    cm_s,
    cm_r,
    vs_s,
    vs_r,
):
    rows, dim = x_h.shape
    images = rows // SEQ
    r = qm.shape[1]
    hw = qm.shape[2]
    ff = wts.shape[2]
    fw = am.shape[1]
    half = fw // 2
    slot_rows = wbuf.shape[4]
    heads = dim // HEAD_DIM
    pairs = heads // 2
    t = lax.axis_index("tp")
    d = lax.axis_index("dp")
    l = d // np_
    p = d - l * np_
    o = 1 - t

    def at(ll, pp):
        return {"dp": ll * np_ + pp}

    def line_peer(k):
        return lax.rem(l + k, nl)

    def plane_peer(k):
        return lax.rem(p + k, np_)

    x_in = pltpu.make_async_copy(x_h, gp.at[0:rows, 0:dim], dma_sem.at[0])
    c_in = pltpu.make_async_copy(cot_h, gp.at[0:rows, dim : 2 * dim], dma_sem.at[1])
    x_in.start()
    c_in.start()

    barrier = pltpu.get_barrier_semaphore()
    for k in range(1, nl):
        pl.semaphore_signal(barrier, inc=1, device_id=at(line_peer(k), p), device_id_type=MESH)
    for k in range(1, np_):
        pl.semaphore_signal(barrier, inc=1, device_id=at(l, plane_peer(k)), device_id_type=MESH)
    pl.semaphore_signal(barrier, inc=1, device_id={"tp": o}, device_id_type=MESH)

    tr_a[...] = jnp.zeros_like(tr_a)

    def put_slot(pc, top_parts, bottom_parts):
        at_col = 0
        for part in top_parts:
            pk[0:r, at_col : at_col + part.shape[1]] = part
            at_col += part.shape[1]
        at_col = 0
        for part in bottom_parts:
            pk[r : 2 * r, at_col : at_col + part.shape[1]] = part
            at_col += part.shape[1]
        wbuf[pc, t, p, l] = pk[...].astype(BF16)

    if 2 * r < slot_rows:
        pk[...] = jnp.zeros_like(pk)
    tr_a[0:hw, 0:r] = pm[...]
    tr_b[:, 0:hw] = tr_a[0:hw, :].T
    put_slot(0, (qm[0], qm[1]), (qm[2], tr_b[0:r, 0:hw]))
    put_slot(1, (am[:, 0:half],), (am[:, half:],))
    tr_a[0:fw, 0:r] = cm[...]
    tr_b[...] = tr_a[...].T
    put_slot(2, (tr_b[0:r, 0:half],), (tr_b[0:r, half:],))
    bias2[t] = jnp.broadcast_to(bm[...], bias2.shape[1:])
    keep_all = keep_v[...].astype(F32)
    count = jnp.sum(jnp.sum(keep_all, axis=1, keepdims=True), axis=0, keepdims=True)
    cntl[l] = jnp.broadcast_to(count, cntl.shape[1:])

    pl.semaphore_wait(barrier, nl - 1 + np_ - 1 + 1)

    def remote(src, dst, ssem, rsem, device):
        return pltpu.make_async_remote_copy(
            src_ref=src, dst_ref=dst, send_sem=ssem, recv_sem=rsem, device_id=device, device_id_type=MESH
        )

    sends = []
    bias_cp = remote(bias2.at[t], bias2.at[t], cm_s.at[0], cm_r.at[0], {"tp": o})
    bias_cp.start()
    sends.append(bias_cp)
    for k in range(1, nl):
        cp = remote(cntl.at[l], cntl.at[l], cn_s.at[k], cn_r.at[k], at(line_peer(k), p))
        cp.start()
        sends.append(cp)
    for pc in range(3):
        for k in range(1, nl):
            cp = remote(
                wbuf.at[pc, t, p, l], wbuf.at[pc, t, p, l], ag_ls.at[pc, k], ag_lr.at[pc, k], at(line_peer(k), p)
            )
            cp.start()
            sends.append(cp)

    def got(dst, rsem):
        return remote(dst, dst, dma_sem.at[2], rsem, {"tp": o})

    def line_done(pc):
        for k in range(1, nl):
            src_l = lax.rem(l + nl - k, nl)
            got(wbuf.at[pc, t, p, src_l], ag_lr.at[pc, k]).wait_recv()
        for k in range(1, np_):
            cp = remote(wbuf.at[pc, t, p], wbuf.at[pc, t, p], ag_ps.at[pc, k], ag_pr.at[pc, k], at(l, plane_peer(k)))
            cp.start()
            sends.append(cp)
        cp = remote(wbuf.at[pc, t, p], wbuf.at[pc, t, p], ag_ss.at[pc, 0], ag_sr.at[pc, 0], {"tp": o})
        cp.start()
        sends.append(cp)

    def plane_done(pc):
        for k in range(1, np_):
            src_p = lax.rem(p + np_ - k, np_)
            got(wbuf.at[pc, t, src_p], ag_pr.at[pc, k]).wait_recv()
            cp = remote(wbuf.at[pc, t, src_p], wbuf.at[pc, t, src_p], ag_ss.at[pc, k], ag_sr.at[pc, k], {"tp": o})
            cp.start()
            sends.append(cp)

    def sibling_done(pc):
        for k in range(np_):
            src_p = lax.rem(p + np_ - k, np_)
            got(wbuf.at[pc, o, src_p], ag_sr.at[pc, k]).wait_recv()

    def cols_of(pc, tt):
        if pc == 0:
            return (
                (0, hw, hw * tt),
                (hw, hw, dim + hw * tt),
            ), (
                (0, hw, 2 * dim + hw * tt),
                (hw, hw, 3 * dim + hw * tt),
            )
        return ((0, half, fw * tt),), ((0, half, fw * tt + half),)

    def assemble(pc):
        for tt in range(2):
            top, bottom = cols_of(pc, tt)
            for ll in range(nl):
                for pp in range(np_):
                    slot = wbuf[pc, tt, pp, ll].astype(F32)
                    row = (ll * np_ + pp) * r
                    for base, parts in ((0, top), (r, bottom)):
                        for at_slot, width, at_col in parts:
                            grd[row : row + r, at_col : at_col + width] = slot[
                                base : base + r, at_slot : at_slot + width
                            ]
        wts[pc] = grd[...].astype(BF16)

    def cast_in(col):
        def step(c, carry):
            at_row = pl.ds(pl.multiple_of(c * 16, 16), 16)
            stage[at_row, :] = gp[at_row, col : col + dim].astype(F32)
            return carry

        lax.fori_loop(0, rows // 16, step, 0)

    stage[rows:, :] = jnp.zeros((stage.shape[0] - rows, dim), F32)
    own_keep = keep_v[pl.ds(pl.multiple_of(t * images, images), images), :].astype(F32)
    mkt[...] = jnp.zeros_like(mkt)
    mkt[0:images, 0:SEQ] = own_keep
    keep_t = mkt[...].T
    for i in range(images):
        mcol[i] = jnp.broadcast_to(keep_t[0:PAD, i : i + 1], (PAD, 128))
    inside = lax.broadcasted_iota(jnp.int32, (PAD, dim), 0) < SEQ
    x_in.wait()
    cast_in(0)
    gain1, shift1 = nm[0:1, :], nm[1:2, :]
    for i in range(images):
        v = jnp.where(inside, stage[i * SEQ : i * SEQ + PAD, :], 0.0)
        xpad[i * PAD : (i + 1) * PAD, :] = v.astype(BF16)
        xhat, _ = norm_parts(v)
        n1[i * PAD : (i + 1) * PAD, :] = (xhat * gain1 + shift1).astype(BF16)
    line_done(0)
    c_in.wait()
    cast_in(dim)
    for i in range(images):
        v = jnp.where(inside, stage[i * SEQ : i * SEQ + PAD, :], 0.0)
        m = mcol[i]
        back[i * PAD : (i + 1) * PAD, :] = (v * jnp.concatenate([m] * (dim // 128), axis=1)).astype(BF16)
    line_done(1)
    for k in range(1, nl):
        src_l = lax.rem(l + nl - k, nl)
        got(cntl.at[src_l], cn_r.at[k]).wait_recv()
    cntp[p] = functools.reduce(lambda a, b: a + b, [cntl[ll] for ll in range(nl)])
    for k in range(1, np_):
        cp = remote(cntp.at[p], cntp.at[p], cm_s.at[k], cm_r.at[k], at(l, plane_peer(k)))
        cp.start()
        sends.append(cp)
    line_done(2)
    plane_done(0)
    sibling_done(0)
    got(bias2.at[o], cm_r.at[0]).wait_recv()
    assemble(0)
    for k in range(1, np_):
        src_p = lax.rem(p + np_ - k, np_)
        got(cntp.at[src_p], cm_r.at[k]).wait_recv()
    kept = functools.reduce(lambda a, b: a + b, [cntp[pp] for pp in range(np_)])
    grad_scale = (rows * 2.0 * nl * np_) / kept[0:1, 0:1]

    def image_rows(i):
        return pl.ds(pl.multiple_of(i * PAD, 16), PAD)

    q_bias = jnp.concatenate([bias2[0, 0:1, 0:hw], bias2[1, 0:1, 0:hw]], axis=1)
    v_bias = jnp.concatenate([bias2[0, 0:1, hw : 2 * hw], bias2[1, 0:1, hw : 2 * hw]], axis=1)
    h_bias = jnp.concatenate([bias2[0, 0:1, 2 * hw :], bias2[1, 0:1, 2 * hw :]], axis=1)
    qkv_bias = jnp.concatenate([q_bias, jnp.zeros_like(q_bias), v_bias], axis=1)

    def qkv_step(i, carry):
        here = image_rows(i)
        v = n1[here, :]
        for c in range(3):
            cols = slice(c * dim, (c + 1) * dim)
            qkv[here, cols] = (dot_nn(v, wts[0, :, cols]) + qkv_bias[:, cols]).astype(BF16)
        return carry

    lax.fori_loop(0, images, qkv_step, 0)
    plane_done(1)

    lane = lax.broadcasted_iota(jnp.int32, (1, 128), 1)
    head_mask = [(lane < HEAD_DIM).astype(F32).astype(BF16), (lane >= HEAD_DIM).astype(F32).astype(BF16)]

    def attend_step(i, carry):
        here = image_rows(i)
        m = mcol[i]
        m = jnp.concatenate([m, m], axis=1)[:, 0:PAD] > 0.0
        for c in range(pairs):
            qp = qkv[here, c * 128 : (c + 1) * 128]
            kp = qkv[here, dim + c * 128 : dim + (c + 1) * 128]
            vp = qkv[here, 2 * dim + c * 128 : 2 * dim + (c + 1) * 128]
            total = None
            for h in range(2):
                s = dot_nt(kp * head_mask[h], qp) * SCALE
                s = jnp.where(m, s, NEG)
                e = jnp.exp(s - jnp.max(s, axis=0, keepdims=True))
                pr = e * (1.0 / jnp.sum(e, axis=0, keepdims=True))
                probs[i * heads + 2 * c + h] = pr
                term = dot_tn(pr.astype(BF16), vp * head_mask[h])
                total = term if total is None else total + term
            att[here, c * 128 : (c + 1) * 128] = total.astype(BF16)
        return carry

    lax.fori_loop(0, images, attend_step, 0)
    plane_done(2)
    sibling_done(1)
    sibling_done(2)
    assemble(1)
    assemble(2)
    for cp in sends:
        cp.wait_send()

    vec[...] = jnp.zeros_like(vec)
    bias4, gain2, shift2, bias5 = nm[4:5, :], nm[2:3, :], nm[3:4, :], nm[5:6, :]
    chunk = 512

    def ff_step(i, carry):
        here = image_rows(i)
        proj_t = wts[0, :, 3 * dim : 4 * dim]
        m = xpad[here, :].astype(F32) + (dot_nt(att[here, :], proj_t) + bias4)
        xhat, rstd = norm_parts(m)
        normed = (xhat * gain2 + shift2).astype(BF16)
        n2[here, :] = normed
        b = back[here, :]
        for j in range(ff // chunk):
            cols = slice(j * chunk, (j + 1) * chunk)
            pre = dot_nn(normed, wts[1, :, cols]) + h_bias[:, cols]
            ga = dot_nn(b, wts[2, :, cols])
            value, slope = gelu_parts(pre)
            act[here, cols] = value.astype(BF16)
            gpre = (ga * slope).astype(BF16)
            gp[here, cols] = gpre
            sums = jnp.sum(gpre.astype(F32), axis=0, keepdims=True)
            vec[8:9, cols] += sums
        opad[here, :] = (m + (dot_nt(act[here, :], wts[2]) + bias5)).astype(BF16)
        dn = dot_nt(gp[here, :], wts[1])
        bfl = b.astype(F32)
        gm = bfl + norm_back(dn, xhat, rstd, gain2)
        mid[here, :] = gm
        g16 = gm.astype(BF16)
        gbr[here, :] = g16
        gatt[here, :] = dot_nn(g16, proj_t).astype(BF16)
        vec[2:3, 0:dim] += jnp.sum(dn * xhat, axis=0, keepdims=True)
        vec[3:4, 0:dim] += jnp.sum(dn, axis=0, keepdims=True)
        vec[4:5, 0:dim] += jnp.sum(g16.astype(F32), axis=0, keepdims=True)
        vec[5:6, 0:dim] += jnp.sum(bfl, axis=0, keepdims=True)
        return carry

    lax.fori_loop(0, images, ff_step, 0)

    def pack(pc):
        for tt in range(2):
            top, bottom = cols_of(pc, tt)
            for ll in range(nl):
                for pp in range(np_):
                    row = (ll * np_ + pp) * r
                    for base, parts in ((0, top), (r, bottom)):
                        for at_slot, width, at_col in parts:
                            pk[base : base + r, at_slot : at_slot + width] = grd[
                                row : row + r, at_col : at_col + width
                            ]
                    wbuf[pc, tt, pp, ll] = pk[...].astype(BF16)

    sib_sends = {}

    def send_sibling(pc):
        cp = remote(wbuf.at[pc, o], sib.at[pc], rs_ss.at[pc], rs_sr.at[pc], {"tp": o})
        cp.start()
        sib_sends[pc] = cp

    late = []

    def send_plane(pc):
        got(sib.at[pc], rs_sr.at[pc]).wait_recv()
        for pp in range(np_):
            for ll in range(nl):
                sib[pc, pp, ll] = (sib[pc, pp, ll].astype(F32) + wbuf[pc, t, pp, ll].astype(F32)).astype(BF16)
        for k in range(1, np_):
            cp = remote(
                sib.at[pc, plane_peer(k)], rpl.at[pc, p], rs_ps.at[pc, k], rs_pr.at[pc, k], at(l, plane_peer(k))
            )
            cp.start()
            late.append(cp)
        rpl[pc, p] = sib[pc, p]

    def send_line(pc):
        for k in range(1, np_):
            src_p = lax.rem(p + np_ - k, np_)
            got(rpl.at[pc, src_p], rs_pr.at[pc, k]).wait_recv()
        for ll in range(nl):
            lsn[pc, ll] = functools.reduce(
                lambda a, b: a + b, [rpl[pc, pp, ll].astype(F32) for pp in range(np_)]
            ).astype(BF16)
        for k in range(1, nl):
            cp = remote(
                lsn.at[pc, line_peer(k)], rln.at[pc, l], rs_ls.at[pc, k], rs_lr.at[pc, k], at(line_peer(k), p)
            )
            cp.start()
            late.append(cp)
        rln[pc, l] = lsn[pc, l]

    def sum_line(pc):
        for k in range(1, nl):
            src_l = lax.rem(l + nl - k, nl)
            got(rln.at[pc, src_l], rs_lr.at[pc, k]).wait_recv()
        fin[pc] = functools.reduce(lambda a, b: a + b, [rln[pc, ll].astype(F32) for ll in range(nl)])

    def grad_step(left, right, width):
        def step(j, carry):
            cols = pl.ds(pl.multiple_of(j * 256, 256), 256)
            grd[:, cols] = dot_tn(left[...], right[:, cols])
            return carry

        lax.fori_loop(0, width // 256, step, 0)

    grad_step(back, act, ff)
    pack(2)
    send_sibling(2)
    grad_step(n2, gp, ff)
    pack(1)
    send_sibling(1)
    send_plane(2)
    grd[:, 3 * dim :] = dot_tn(gbr[...], att[...])
    send_plane(1)
    send_line(2)

    def attend_back(i, carry):
        here = image_rows(i)
        for c in range(pairs):
            qp = qkv[here, c * 128 : (c + 1) * 128]
            kp = qkv[here, dim + c * 128 : dim + (c + 1) * 128]
            vp = qkv[here, 2 * dim + c * 128 : 2 * dim + (c + 1) * 128]
            da = gatt[here, c * 128 : (c + 1) * 128]
            dq = dk = dv = 0.0
            for h in range(2):
                hm = head_mask[h]
                pr = probs[i * heads + 2 * c + h]
                dp = dot_nt(vp * hm, da)
                inner = jnp.sum(pr * dp, axis=0, keepdims=True)
                ds = (pr * (dp - inner)).astype(BF16)
                dv = dv + dot_nn(pr.astype(BF16), da * hm)
                dk = dk + dot_nn(ds, qp * hm)
                dq = dq + dot_tn(ds, kp * hm)
            dq = (dq * SCALE).astype(BF16)
            dv = dv.astype(BF16)
            act[here, c * 128 : (c + 1) * 128] = dq
            act[here, dim + c * 128 : dim + (c + 1) * 128] = (dk * SCALE).astype(BF16)
            act[here, 2 * dim + c * 128 : 2 * dim + (c + 1) * 128] = dv
            vec[6:7, c * 128 : (c + 1) * 128] += jnp.sum(dq.astype(F32), axis=0, keepdims=True)
            vec[7:8, c * 128 : (c + 1) * 128] += jnp.sum(dv.astype(F32), axis=0, keepdims=True)
        return carry

    lax.fori_loop(0, images, attend_back, 0)
    send_line(1)

    def qkv_grad(j, carry):
        cols = pl.ds(pl.multiple_of(j * 384, 128), 384)
        grd[:, cols] = dot_tn(n1[...], act[:, cols])
        return carry

    lax.fori_loop(0, 3, qkv_grad, 0)
    pack(0)
    send_sibling(0)

    def last_step(i, carry):
        here = image_rows(i)
        dn = dot_nt(act[here, 0 : 3 * dim], wts[0, :, 0 : 3 * dim])
        xhat, rstd = norm_parts(xpad[here, :].astype(F32))
        mid[here, :] = (mid[here, :] + norm_back(dn, xhat, rstd, gain1)) * grad_scale
        vec[0:1, 0:dim] += jnp.sum(dn * xhat, axis=0, keepdims=True)
        vec[1:2, 0:dim] += jnp.sum(dn, axis=0, keepdims=True)
        return carry

    lax.fori_loop(0, images, last_step, 0)
    vec_cp = remote(vec, vsib, vs_s.at[0], vs_r.at[0], {"tp": o})
    vec_cp.start()
    send_plane(0)

    for i in range(images):
        stage[i * SEQ : (i + 1) * SEQ, :] = opad[i * PAD : i * PAD + SEQ, :].astype(F32)

    def cast_out(c, carry):
        at_row = pl.ds(pl.multiple_of(c * 16, 16), 16)
        gp[at_row, 0:dim] = stage[at_row, :].astype(BF16)
        return carry

    lax.fori_loop(0, rows // 16, cast_out, 0)
    out_cp = pltpu.make_async_copy(gp.at[0:rows, 0:dim], out_h, dma_sem.at[0])
    out_cp.start()
    got(vsib, vs_r.at[0]).wait_recv()
    vpl[p] = vec[...] + vsib[...]
    for k in range(1, np_):
        cp = remote(vpl.at[p], vpl.at[p], vs_s.at[k], vs_r.at[k], at(l, plane_peer(k)))
        cp.start()
        late.append(cp)
    for i in range(images):
        stage[i * SEQ : (i + 1) * SEQ, :] = mid[i * PAD : i * PAD + SEQ, :]
    gin_cp = pltpu.make_async_copy(stage.at[0:rows, :], gin_h, dma_sem.at[1])
    gin_cp.start()
    for k in range(1, np_):
        src_p = lax.rem(p + np_ - k, np_)
        got(vpl.at[src_p], vs_r.at[k]).wait_recv()
    vln[l] = functools.reduce(lambda a, b: a + b, [vpl[pp] for pp in range(np_)])
    for k in range(1, nl):
        cp = remote(vln.at[l], vln.at[l], vs_s.at[np_ + k], vs_r.at[np_ + k], at(line_peer(k), p))
        cp.start()
        late.append(cp)
    send_line(0)

    def update(grad, m_in, f_in, s_in, f_out, s_out, m_out, c_out, rate, decay):
        first, second, master = adam(m_in, f_in, s_in, grad * grad_scale, rate, decay)
        f_out[...] = first
        s_out[...] = second
        m_out[...] = master
        if c_out is not None:
            c_out[...] = master.astype(BF16)

    sum_line(1)
    update(
        jnp.concatenate([fin[1, 0:r, :], fin[1, r : 2 * r, :]], axis=1),
        am[...], af[...], as_[...], af_o, as_o, am_o, ac_o, 0.08, matrix_decay,
    )
    sum_line(2)
    tr_b[0:r, 0:half] = fin[2, 0:r, :]
    tr_b[0:r, half:] = fin[2, r : 2 * r, :]
    tr_a[...] = tr_b[...].T
    update(
        tr_a[0:fw, 0:r], cm[...], cf[...], cs[...], cf_o, cs_o, cm_o, cc_o, 0.04, matrix_decay
    )
    for k in range(1, nl):
        src_l = lax.rem(l + nl - k, nl)
        got(vln.at[src_l], vs_r.at[np_ + k]).wait_recv()
    vec_cp.wait_send()
    vec[...] = functools.reduce(lambda a, b: a + b, [vln[ll] for ll in range(nl)])
    update(vec[0:6, 0:dim], nm[...], nf[...], ns[...], nf_o, ns_o, nm_o, None, 0.5, 0.0)
    own = t == 0

    def pick(row, width):
        return jnp.where(own, vec[row : row + 1, 0:width], vec[row : row + 1, width : 2 * width])

    update(
        jnp.concatenate([pick(6, hw), pick(7, hw), pick(8, fw)], axis=1),
        bm[...], bf[...], bs[...], bf_o, bs_o, bm_o, None, 0.5, 0.0,
    )
    sum_line(0)
    g0 = fin[0]
    for c, grad in enumerate((g0[0:r, 0:hw], g0[0:r, hw:], g0[r : 2 * r, 0:hw])):
        update(
            grad, qm[c], qf[c], qs[c], qf_o.at[c], qs_o.at[c], qm_o.at[c], qc_o.at[c], 0.08, matrix_decay
        )
    tr_b[0:r, 0:hw] = g0[r : 2 * r, hw:]
    tr_a[0:hw, :] = tr_b[:, 0:hw].T
    update(tr_a[0:hw, 0:r], pm[...], pf[...], ps[...], pf_o, ps_o, pm_o, pc_o, 0.8, matrix_decay)

    out_cp.wait()
    gin_cp.wait()
    for cp in late:
        cp.wait_send()
    for cp in sib_sends.values():
        cp.wait_send()


def body(
    inputs, keep_mask, cotangent,
    qkv_master, qkv_first, qkv_second,
    proj_master, proj_first, proj_second,
    fc1_master, fc1_first, fc1_second,
    fc2_master, fc2_first, fc2_second,
    norm_master, norm_first, norm_second,
    bias_master, bias_first, bias_second,
):
    n = lax.axis_size("dp")
    nl = 4 if n % 4 == 0 else n
    np_ = n // nl
    rows, dim = inputs.shape
    images = rows // SEQ
    padded = images * PAD
    r = qkv_master.shape[1]
    hw = qkv_master.shape[2]
    fw = fc1_master.shape[1]
    ff = 2 * fw
    slot = -(-2 * r // 16) * 16
    keep = keep_mask.reshape(2 * images, SEQ)
    vm = pl.BlockSpec(memory_space=pltpu.VMEM)
    hbm = pl.BlockSpec(memory_space=pl.ANY)

    def like(a, dtype=None):
        return jax.ShapeDtypeStruct(a.shape, dtype or a.dtype)

    outs = [like(inputs), like(inputs, F32)]
    for a in (qkv_master, proj_master, fc1_master, fc2_master):
        outs += [like(a), like(a), like(a), like(a, BF16)]
    for a in (norm_master, bias_master):
        outs += [like(a)] * 3
    dma = pltpu.SemaphoreType.DMA
    scratch = [
        pltpu.VMEM((3, 2, np_, nl, slot, dim), BF16),
        pltpu.VMEM((3, dim, ff), BF16),
        pltpu.VMEM((dim, ff), F32),
        pltpu.VMEM((3, np_, nl, slot, dim), BF16),
        pltpu.VMEM((3, np_, nl, slot, dim), BF16),
        pltpu.VMEM((3, nl, slot, dim), BF16),
        pltpu.VMEM((3, nl, slot, dim), BF16),
        pltpu.VMEM((3, slot, dim), F32),
        pltpu.VMEM((slot, dim), F32),
        pltpu.VMEM((fw, 128), F32),
        pltpu.VMEM((128, fw), F32),
        pltpu.VMEM((2, 8, bias_master.shape[1]), F32),
        pltpu.VMEM((nl, 8, 128), F32),
        pltpu.VMEM((np_, 8, 128), F32),
        pltpu.VMEM((16, ff), F32),
        pltpu.VMEM((16, ff), F32),
        pltpu.VMEM((np_, 16, ff), F32),
        pltpu.VMEM((nl, 16, ff), F32),
        pltpu.VMEM((-(-(rows - SEQ + PAD) // 16) * 16, dim), F32),
        pltpu.VMEM((padded, dim), F32),
        pltpu.VMEM((images * (dim // HEAD_DIM), PAD, PAD), F32),
        pltpu.VMEM((images, PAD, 128), F32),
        pltpu.VMEM((128, 256), F32),
        pltpu.VMEM((padded, dim), BF16),
        pltpu.VMEM((padded, dim), BF16),
        pltpu.VMEM((padded, dim), BF16),
        pltpu.VMEM((padded, 3 * dim), BF16),
        pltpu.VMEM((padded, dim), BF16),
        pltpu.VMEM((padded, dim), BF16),
        pltpu.VMEM((padded, dim), BF16),
        pltpu.VMEM((padded, dim), BF16),
        pltpu.VMEM((padded, dim), BF16),
        pltpu.VMEM((padded, ff), BF16),
        pltpu.VMEM((padded, ff), BF16),
        dma((3,)),
        dma((1,)),
        dma((3, nl)),
        dma((3, nl)),
        dma((3, np_)),
        dma((3, np_)),
        dma((3, np_)),
        dma((3, np_)),
        dma((3,)),
        dma((3,)),
        dma((3, np_)),
        dma((3, np_)),
        dma((3, nl)),
        dma((3, nl)),
        dma((nl,)),
        dma((nl,)),
        dma((np_,)),
        dma((np_,)),
        dma((np_ + nl,)),
        dma((np_ + nl,)),
    ]
    return pl.pallas_call(
        functools.partial(kernel, nl, np_),
        out_shape=outs,
        in_specs=[hbm, vm, hbm] + [vm] * 18,
        out_specs=[hbm, hbm] + [vm] * 22,
        scratch_shapes=scratch,
        compiler_params=pltpu.CompilerParams(
            collective_id=0, has_side_effects=True, vmem_limit_bytes=64 * 1024 * 1024
        ),
    )(
        inputs, keep, cotangent,
        qkv_master, qkv_first, qkv_second,
        proj_master, proj_first, proj_second,
        fc1_master, fc1_first, fc1_second,
        fc2_master, fc2_first, fc2_second,
        norm_master, norm_first, norm_second,
        bias_master, bias_first, bias_second,
    )


def solution(mesh):
    mats = [P(None, "dp", "tp"), P("tp", "dp"), P("dp", "tp"), P("tp", "dp")]
    in_specs = [P(("dp", "tp"), None), P("dp"), P(("dp", "tp"), None)]
    out_specs = [P(("dp", "tp"), None), P(("dp", "tp"), None)]
    for m in mats:
        in_specs += [m] * 3
        out_specs += [m] * 4
    in_specs += [P()] * 3 + [P("tp", None)] * 3
    out_specs += [P()] * 3 + [P("tp", None)] * 3
    return jax.shard_map(
        body, mesh=mesh, in_specs=tuple(in_specs), out_specs=tuple(out_specs), check_vma=False
    )
```

time: 613 us -> 168 us (0.27)
  blocking collectives: 210 us -> 0 us
  waiting for transfers between devices: 134 us -> 0 us
  Pallas kernels: 0 us -> 132 us
  matrix products: 117 us -> 0 us
  other arithmetic: 64.5 us -> 0 us
  local copies, waits for them, and re-layouts: 66.8 us -> 34.9 us
  between operations: 16.2 us -> 0.8 us
    all_gather x4 -> x0, blocking collectives: 165 us -> none  [the longest x1 43.4 us: body(): lax.all_gather(proj_master.astype(jnp.bfloat16), 'dp', axis=1, tiled=True)]
    psum x4 -> x0, waiting for transfers between devices: 134 us -> none  [the longest x1 111 us: body(): lax.psum((matrix_grads[0], matrix_grads[1], matrix_grads[2], matrix_grads...]
    pallas_call x0 -> x1, Pallas kernels: none -> 132 us  [body(): pl.pallas_call(functools.partial(kernel, nl, np_), out_shape=outs, in_spe...]
    dot_general x20 -> x0, matrix products: 117 us -> none  [the longest x1 26.4 us: body(): jnp.dot(normed2, fc1_weight, preferred_element_type=jnp.float32)]
    psum x1 -> x0, blocking collectives: 45 us -> none  [body(): lax.psum((vector_grad, bias_grid, jnp.sum(local_kept)), ('dp', 'tp'))]
    reduce_sum x11 -> x0, other arithmetic: 37.9 us -> none  [the longest x2 13.1 us: normalize(): centred = values_in - row_mean]
    reshape x8 -> x1, local copies, waits for them, and re-layouts: 24.8 us -> 1.45 us  [body(): keep = keep_mask.reshape(2 * images, SEQ)]
    convert_element_type x12 -> x0, other arithmetic: 20.2 us -> none  [the longest x4 6.21 us: body(): outputs.append(new_master.astype(jnp.bfloat16))]
  transfers between devices with their start and end apart: 7 -> 0, of which waited for: 3 -> 0; matrix products, arithmetic and copies ran while one was open for 25% -> 0% of each run, Pallas kernels for 0% -> 0%
where the time goes in v1:
time: 168 us
  Pallas kernels  132 us (79%)
  local copies, waits for them, and re-layouts  34.9 us (21%)
    pallas_call x1, Pallas kernels, body(): pl.pallas_call(functools.partial(kernel, nl, np_), out_shape=outs, in_spe...  132 us
    unnamed x58, local copies, waits for them, and re-layouts  21.2 us
    pallas_call x8, local copies, waits for them, and re-layouts, body(): pl.pallas_call(functools.partial(kernel, nl, np_), out_shape=outs, in_spe...  12.3 us

profile of v1, /device:TPU:0, one launch (start us, length us, event | category | flops | bytes accessed | tf_op | source)
XLA Modules:
  0.0 167.6 jit_solution(1988077170537503597)
XLA Ops:
  0.7 1.5 reshape.51.keep_v
  2.1 1.5 copy.45.pm
  3.6 1.5 copy.46.pf
  5.1 1.5 copy.47.ps
  6.6 1.8 %copy.48.cm = f32[768,24]{1,0:T(8,128)} copy(f32[768,24]{0,1:T(8,128)} %param.33) | data formatting | bytes 147456 | tf_op args[12]
  8.4 1.8 %copy.49.cf = f32[768,24]{1,0:T(8,128)} copy(f32[768,24]{0,1:T(8,128)} %param.34) | data formatting | bytes 147456 | tf_op args[13]
  10.2 0.9 copy.50.cs
  11.1 131.8 %shard_map.388 = (bf16[1584,384]{1,0:T(8,128)(2,1)}, f32[1584,384]{1,0:T(8,128)}, f32[3,24,192]{2,1,0:T(8,128)}, f32[3,24,192]{2,1,0:T(8,128)}, f32[3,24,192]{2,...) custom-call(bf16[1584,384]{1,0:T(8,128)(2,1)} %x_h.1, ...), custom_call_target="tpu_custom_call" | custom-call | tf_op jit(solution)/shard_map/pallas_call | solution.py:767
  143.0 1.6 copy.54
  144.6 1.6 copy.51
  146.1 1.6 copy.52
  147.7 1.6 copy.53
  149.3 1.7 copy.58
  150.9 1.8 %copy.55 = f32[768,24]{0,1:T(8,128)} copy(f32[768,24]{1,0:T(8,128)} %get-tuple-element.38) | data formatting | bytes 147456 | tf_op jit(solution)/shard_map/pallas_call | solution.py:767
  152.7 1.8 %copy.56 = f32[768,24]{0,1:T(8,128)} copy(f32[768,24]{1,0:T(8,128)} %get-tuple-element.39) | data formatting | bytes 147456 | tf_op jit(solution)/shard_map/pallas_call | solution.py:767
  154.5 0.8 copy.57
  155.2 1.0 copy.75
  156.3 1.1 copy-done
  157.5 1.4 copy.76
  158.9 0.6 copy.77
  159.6 0.6 copy.78
  160.2 0.6 copy.79
  161.4 0.6 copy.81
  162.1 0.6 copy.82
  (44 shorter events, 5.5 us)
Async XLA Ops:
  0.7 9.5 %copy-start.3 = (f32[768,24]{0,1:T(8,128)S(1)}, f32[768,24]{0,1:T(8,128)}, u32[]{:S(2)}) copy-start(f32[768,24]{0,1:T(8,128)} %param.35) | copy-start | bytes 221188
  142.9 11.5 %copy-start.2 = (f32[768,24]{1,0:T(8,128)S(1)}, f32[768,24]{1,0:T(8,128)}, u32[]{:S(2)}) copy-start(f32[768,24]{1,0:T(8,128)} %get-tuple-element.40) | copy-start | bytes 221188
  143.0 12.3 %copy-start.1 = (bf16[1584,384]{1,0:T(8,128)(2,1)S(1)}, bf16[1584,384]{1,0:T(8,128)(2,1)}, u32[]{:S(2)}) copy-start(bf16[1584,384]{1,0:T(8,128)(2,1)} %get-tuple-element.72) | copy-start | bytes 3649540
  155.2 2.1 %copy-start = (f32[1584,384]{1,0:T(8,128)S(1)}, f32[1584,384]{1,0:T(8,128)}, u32[]{:S(2)}) copy-start(f32[1584,384]{1,0:T(8,128)} %get-tuple-element.73) | copy-start | bytes 7299076
  157.4 1.5 copy-start.9
  157.4 2.2 %copy-start.8 = (f32[3,24,192]{2,1,0:T(8,128)S(1)}, f32[3,24,192]{2,1,0:T(8,128)}, u32[]{:S(2)}) copy-start(f32[3,24,192]{2,1,0:T(8,128)} %get-tuple-element.75) | copy-start | bytes 165892
  157.4 2.8 %copy-start.7 = (f32[3,24,192]{2,1,0:T(8,128)S(1)}, f32[3,24,192]{2,1,0:T(8,128)}, u32[]{:S(2)}) copy-start(f32[3,24,192]{2,1,0:T(8,128)} %get-tuple-element.76) | copy-start | bytes 165892
  157.4 3.4 %copy-start.11 = (bf16[3,24,192]{2,1,0:T(8,128)(2,1)S(1)}, bf16[3,24,192]{2,1,0:T(8,128)(2,1)}, u32[]{:S(2)}) copy-start(bf16[3,24,192]{2,1,0:T(8,128)(2,1)} %get-tuple-element.77) | copy-start | bytes 82948
  157.4 4.1 %copy-start.6 = (f32[24,768]{1,0:T(8,128)S(1)}, f32[24,768]{1,0:T(8,128)}, u32[]{:S(2)}) copy-start(f32[24,768]{1,0:T(8,128)} %get-tuple-element.82) | copy-start | bytes 221188
  157.4 4.7 %copy-start.5 = (f32[24,768]{1,0:T(8,128)S(1)}, f32[24,768]{1,0:T(8,128)}, u32[]{:S(2)}) copy-start(f32[24,768]{1,0:T(8,128)} %get-tuple-element.83) | copy-start | bytes 221188
  157.4 5.3 %copy-start.4 = (f32[24,768]{1,0:T(8,128)S(1)}, f32[24,768]{1,0:T(8,128)}, u32[]{:S(2)}) copy-start(f32[24,768]{1,0:T(8,128)} %get-tuple-element.84) | copy-start | bytes 221188
  157.4 5.9 %copy-start.10 = (bf16[24,768]{1,0:T(8,128)(2,1)S(1)}, bf16[24,768]{1,0:T(8,128)(2,1)}, u32[]{:S(2)}) copy-start(bf16[24,768]{1,0:T(8,128)(2,1)} %get-tuple-element.85) | copy-start | bytes 110596
  157.4 6.5 %copy-start.14 = (f32[6,384]{1,0:T(8,128)S(1)}, f32[6,384]{1,0:T(8,128)}, u32[]{:S(2)}) copy-start(f32[6,384]{1,0:T(8,128)} %get-tuple-element.90) | copy-start | bytes 27652
  157.4 7.1 %copy-start.13 = (f32[6,384]{1,0:T(8,128)S(1)}, f32[6,384]{1,0:T(8,128)}, u32[]{:S(2)}) copy-start(f32[6,384]{1,0:T(8,128)} %get-tuple-element.91) | copy-start | bytes 27652
  157.4 7.7 %copy-start.12 = (f32[6,384]{1,0:T(8,128)S(1)}, f32[6,384]{1,0:T(8,128)}, u32[]{:S(2)}) copy-start(f32[6,384]{1,0:T(8,128)} %get-tuple-element.92) | copy-start | bytes 27652
  157.5 8.3 %copy-start.17 = (f32[1,1152]{1,0:T(1,128)S(1)}, f32[1,1152]{1,0:T(1,128)}, u32[]{:S(2)}) copy-start(f32[1,1152]{1,0:T(1,128)} %get-tuple-element.93) | copy-start | bytes 13828
  157.5 8.9 %copy-start.16 = (f32[1,1152]{1,0:T(1,128)S(1)}, f32[1,1152]{1,0:T(1,128)}, u32[]{:S(2)}) copy-start(f32[1,1152]{1,0:T(1,128)} %get-tuple-element.94) | copy-start | bytes 13828
  157.5 9.5 %copy-start.15 = (f32[1,1152]{1,0:T(1,128)S(1)}, f32[1,1152]{1,0:T(1,128)}, u32[]{:S(2)}) copy-start(f32[1,1152]{1,0:T(1,128)} %get-tuple-element.95) | copy-start | bytes 13828

commit v2 on v1

--- a/solution.py
+++ b/solution.py
@@ -87,47 +87,16 @@
     keep_v,
     cot_h,
     qm,
-    qf,
-    qs,
     pm,
-    pf,
-    ps,
     am,
-    af,
-    as_,
     cm,
-    cf,
-    cs,
     nm,
-    nf,
-    ns,
     bm,
-    bf,
-    bs,
     out_h,
     gin_h,
-    qf_o,
-    qs_o,
-    qm_o,
-    qc_o,
-    pf_o,
-    ps_o,
-    pm_o,
-    pc_o,
-    af_o,
-    as_o,
-    am_o,
-    ac_o,
-    cf_o,
-    cs_o,
-    cm_o,
-    cc_o,
-    nf_o,
-    ns_o,
-    nm_o,
-    bf_o,
-    bs_o,
-    bm_o,
+    fin,
+    vec_o,
+    kept_o,
     wbuf,
     wts,
     grd,
@@ -135,10 +104,7 @@
     rpl,
     lsn,
     rln,
-    fin,
     pk,
-    tr_a,
-    tr_b,
     bias2,
     cntl,
     cntp,
@@ -220,8 +186,6 @@
         pl.semaphore_signal(barrier, inc=1, device_id=at(l, plane_peer(k)), device_id_type=MESH)
     pl.semaphore_signal(barrier, inc=1, device_id={"tp": o}, device_id_type=MESH)
 
-    tr_a[...] = jnp.zeros_like(tr_a)
-
     def put_slot(pc, top_parts, bottom_parts):
         at_col = 0
         for part in top_parts:
@@ -235,13 +199,9 @@
 
     if 2 * r < slot_rows:
         pk[...] = jnp.zeros_like(pk)
-    tr_a[0:hw, 0:r] = pm[...]
-    tr_b[:, 0:hw] = tr_a[0:hw, :].T
-    put_slot(0, (qm[0], qm[1]), (qm[2], tr_b[0:r, 0:hw]))
+    put_slot(0, (qm[0], qm[1]), (qm[2], pm[...]))
     put_slot(1, (am[:, 0:half],), (am[:, half:],))
-    tr_a[0:fw, 0:r] = cm[...]
-    tr_b[...] = tr_a[...].T
-    put_slot(2, (tr_b[0:r, 0:half],), (tr_b[0:r, half:],))
+    put_slot(2, (cm[:, 0:half],), (cm[:, half:],))
     bias2[t] = jnp.broadcast_to(bm[...], bias2.shape[1:])
     keep_all = keep_v[...].astype(F32)
     count = jnp.sum(jnp.sum(keep_all, axis=1, keepdims=True), axis=0, keepdims=True)
@@ -622,57 +582,79 @@
         late.append(cp)
     send_line(0)
 
-    def update(grad, m_in, f_in, s_in, f_out, s_out, m_out, c_out, rate, decay):
-        first, second, master = adam(m_in, f_in, s_in, grad * grad_scale, rate, decay)
-        f_out[...] = first
-        s_out[...] = second
-        m_out[...] = master
-        if c_out is not None:
-            c_out[...] = master.astype(BF16)
-
-    sum_line(1)
-    update(
-        jnp.concatenate([fin[1, 0:r, :], fin[1, r : 2 * r, :]], axis=1),
-        am[...], af[...], as_[...], af_o, as_o, am_o, ac_o, 0.08, matrix_decay,
-    )
-    sum_line(2)
-    tr_b[0:r, 0:half] = fin[2, 0:r, :]
-    tr_b[0:r, half:] = fin[2, r : 2 * r, :]
-    tr_a[...] = tr_b[...].T
-    update(
-        tr_a[0:fw, 0:r], cm[...], cf[...], cs[...], cf_o, cs_o, cm_o, cc_o, 0.04, matrix_decay
-    )
     for k in range(1, nl):
         src_l = lax.rem(l + nl - k, nl)
         got(vln.at[src_l], vs_r.at[np_ + k]).wait_recv()
+    vec_o[...] = functools.reduce(lambda a, b: a + b, [vln[ll] for ll in range(nl)])
+    kept_o[...] = kept
+    sum_line(1)
+    sum_line(2)
+    sum_line(0)
     vec_cp.wait_send()
-    vec[...] = functools.reduce(lambda a, b: a + b, [vln[ll] for ll in range(nl)])
-    update(vec[0:6, 0:dim], nm[...], nf[...], ns[...], nf_o, ns_o, nm_o, None, 0.5, 0.0)
-    own = t == 0
-
-    def pick(row, width):
-        return jnp.where(own, vec[row : row + 1, 0:width], vec[row : row + 1, width : 2 * width])
-
-    update(
-        jnp.concatenate([pick(6, hw), pick(7, hw), pick(8, fw)], axis=1),
-        bm[...], bf[...], bs[...], bf_o, bs_o, bm_o, None, 0.5, 0.0,
-    )
-    sum_line(0)
-    g0 = fin[0]
-    for c, grad in enumerate((g0[0:r, 0:hw], g0[0:r, hw:], g0[r : 2 * r, 0:hw])):
-        update(
-            grad, qm[c], qf[c], qs[c], qf_o.at[c], qs_o.at[c], qm_o.at[c], qc_o.at[c], 0.08, matrix_decay
-        )
-    tr_b[0:r, 0:hw] = g0[r : 2 * r, hw:]
-    tr_a[0:hw, :] = tr_b[:, 0:hw].T
-    update(tr_a[0:hw, 0:r], pm[...], pf[...], ps[...], pf_o, ps_o, pm_o, pc_o, 0.8, matrix_decay)
-
     out_cp.wait()
     gin_cp.wait()
     for cp in late:
         cp.wait_send()
     for cp in sib_sends.values():
         cp.wait_send()
+
+
+def update_kernel(scale_rows, *refs):
+    fin, vec, kept, out_in, gin_in = refs[:5]
+    states = [refs[5 + 3 * k : 8 + 3 * k] for k in range(6)]
+    out_h, gin_h = refs[23:25]
+    q_o, p_o, a_o, c_o = (refs[25 + 4 * k : 29 + 4 * k] for k in range(4))
+    n_o, b_o = refs[41:44], refs[44:47]
+    out_v, gin_v, sems_in, sems_out = refs[47:]
+    parts = 3
+    size = out_in.shape[0] // parts
+    loads, stores = [], []
+    for k in range(parts):
+        here = pl.ds(k * size, size)
+        for j, (src, via, dst) in enumerate(((out_in, out_v, out_h), (gin_in, gin_v, gin_h))):
+            loads.append(pltpu.make_async_copy(src.at[here, :], via.at[here, :], sems_in.at[j, k]))
+            stores.append(pltpu.make_async_copy(via.at[here, :], dst.at[here, :], sems_out.at[j, k]))
+    for cp in loads:
+        cp.start()
+    for load, store in zip(loads, stores):
+        load.wait()
+        store.start()
+    qkv, proj, fc1, fc2, norm, bias = states
+    r, hw = proj[0].shape
+    fw = fc1[0].shape[1]
+    half = fw // 2
+    grad_scale = scale_rows / kept[0:1, 0:1]
+
+    def update(grad, state, outs, rate, decay, c=None):
+        pick = (lambda ref: ref[...]) if c is None else (lambda ref: ref[c])
+        master, first, second = (pick(ref) for ref in state)
+        first, second, master = adam(master, first, second, grad * grad_scale, rate, decay)
+        for ref, value in zip(outs, (first, second, master, master)):
+            if c is None:
+                ref[...] = value.astype(ref.dtype)
+            else:
+                ref[c] = value.astype(ref.dtype)
+
+    def halves(pc):
+        g = fin[pc]
+        return jnp.concatenate([g[0:r, :], g[r : 2 * r, :]], axis=1)
+
+    g0 = fin[0]
+    update(g0[0:r, 0:hw], qkv, q_o, 0.08, matrix_decay, 0)
+    update(g0[0:r, hw:], qkv, q_o, 0.08, matrix_decay, 1)
+    update(g0[r : 2 * r, 0:hw], qkv, q_o, 0.08, matrix_decay, 2)
+    update(g0[r : 2 * r, hw:], proj, p_o, 0.8, matrix_decay)
+    update(halves(1), fc1, a_o, 0.08, matrix_decay)
+    update(halves(2), fc2, c_o, 0.04, matrix_decay)
+    update(vec[0:6, 0 : norm[0].shape[1]], norm, n_o, 0.5, 0.0)
+    own = lax.axis_index("tp") == 0
+
+    def pick(row, width):
+        return jnp.where(own, vec[row : row + 1, 0:width], vec[row : row + 1, width : 2 * width])
+
+    update(jnp.concatenate([pick(6, hw), pick(7, hw), pick(8, fw)], axis=1), bias, b_o, 0.5, 0.0)
+    for store in stores:
+        store.wait()
 
 
 def body(
@@ -702,11 +684,14 @@
     def like(a, dtype=None):
         return jax.ShapeDtypeStruct(a.shape, dtype or a.dtype)
 
-    outs = [like(inputs), like(inputs, F32)]
-    for a in (qkv_master, proj_master, fc1_master, fc2_master):
-        outs += [like(a), like(a), like(a), like(a, BF16)]
-    for a in (norm_master, bias_master):
-        outs += [like(a)] * 3
+    proj_master, proj_first, proj_second = proj_master.T, proj_first.T, proj_second.T
+    fc2_master, fc2_first, fc2_second = fc2_master.T, fc2_first.T, fc2_second.T
+    large = [like(inputs), like(inputs, F32)]
+    sums = [
+        jax.ShapeDtypeStruct((3, slot, dim), F32),
+        jax.ShapeDtypeStruct((16, ff), F32),
+        jax.ShapeDtypeStruct((8, 128), F32),
+    ]
     dma = pltpu.SemaphoreType.DMA
     scratch = [
         pltpu.VMEM((3, 2, np_, nl, slot, dim), BF16),
@@ -716,10 +701,7 @@
         pltpu.VMEM((3, np_, nl, slot, dim), BF16),
         pltpu.VMEM((3, nl, slot, dim), BF16),
         pltpu.VMEM((3, nl, slot, dim), BF16),
-        pltpu.VMEM((3, slot, dim), F32),
         pltpu.VMEM((slot, dim), F32),
-        pltpu.VMEM((fw, 128), F32),
-        pltpu.VMEM((128, fw), F32),
         pltpu.VMEM((2, 8, bias_master.shape[1]), F32),
         pltpu.VMEM((nl, 8, 128), F32),
         pltpu.VMEM((np_, 8, 128), F32),
@@ -764,24 +746,42 @@
         dma((np_ + nl,)),
         dma((np_ + nl,)),
     ]
-    return pl.pallas_call(
+    out, gin, fin, vec, kept = pl.pallas_call(
         functools.partial(kernel, nl, np_),
-        out_shape=outs,
-        in_specs=[hbm, vm, hbm] + [vm] * 18,
-        out_specs=[hbm, hbm] + [vm] * 22,
+        out_shape=large + sums,
+        in_specs=[hbm, vm, hbm] + [vm] * 6,
+        out_specs=[hbm, hbm] + [vm] * 3,
         scratch_shapes=scratch,
         compiler_params=pltpu.CompilerParams(
             collective_id=0, has_side_effects=True, vmem_limit_bytes=64 * 1024 * 1024
         ),
-    )(
-        inputs, keep, cotangent,
+    )(inputs, keep, cotangent, qkv_master, proj_master, fc1_master, fc2_master, norm_master, bias_master)
+    states = [
         qkv_master, qkv_first, qkv_second,
         proj_master, proj_first, proj_second,
         fc1_master, fc1_first, fc1_second,
         fc2_master, fc2_first, fc2_second,
         norm_master, norm_first, norm_second,
         bias_master, bias_first, bias_second,
+    ]
+    outs = list(large)
+    for a in (qkv_master, proj_master, fc1_master, fc2_master):
+        outs += [like(a), like(a), like(a), like(a, BF16)]
+    for a in (norm_master, bias_master):
+        outs += [like(a)] * 3
+    res = list(
+        pl.pallas_call(
+            functools.partial(update_kernel, rows * 2.0 * n),
+            out_shape=outs,
+            in_specs=[vm] * 3 + [hbm] * 2 + [vm] * 18,
+            out_specs=[hbm] * 2 + [vm] * 22,
+            scratch_shapes=[pltpu.VMEM((rows, dim), BF16), pltpu.VMEM((rows, dim), F32), dma((2, 3)), dma((2, 3))],
+            compiler_params=pltpu.CompilerParams(vmem_limit_bytes=64 * 1024 * 1024),
+        )(fin, vec, kept, out, gin, *states)
     )
+    for k in (6, 7, 8, 9, 14, 15, 16, 17):
+        res[k] = res[k].T
+    return tuple(res)
 
 
 def solution(mesh):

time: 168 us -> 138 us (0.82)
  local copies, waits for them, and re-layouts: 34.9 us -> 1.42 us
  Pallas kernels: 132 us -> 136 us
    unnamed x58 -> x0, local copies, waits for them, and re-layouts: 21.2 us -> none
    pallas_call x8 -> x0, local copies, waits for them, and re-layouts: 12.3 us -> none  [body(): pl.pallas_call(functools.partial(kernel, nl, np_), out_shape=outs, in_spe...]
    pallas_call x1 -> x2, Pallas kernels: 132 us -> 136 us  [the longest x1 130 us: body(): pl.pallas_call(functools.partial(kernel, nl, np_), out_shape=large + sums...]
where the time goes in v2:
time: 138 us
  Pallas kernels  136 us (99%)
  local copies, waits for them, and re-layouts  1.42 us (1%)
    pallas_call x1, Pallas kernels, body(): pl.pallas_call(functools.partial(kernel, nl, np_), out_shape=large + sums...  130 us
    pallas_call x1, Pallas kernels, body(): pl.pallas_call(functools.partial(update_kernel, rows * 2.0 * n), out_shap...  5.54 us

profile of v2, /device:TPU:0, one launch (start us, length us, event | category | flops | bytes accessed | tf_op | source)
XLA Modules:
  0.0 138.0 jit_solution(6345657466463179710)
XLA Ops:
  0.7 1.4 %reshape.51.keep_v = s32[16,198]{1,0:T(8,128)} reshape(s32[3168]{0:T(1024)} %param.22) | data formatting | bytes 25344 | tf_op jit(solution)/shard_map/reshape | solution.py:680
  2.1 130.4 %shard_map.388 = (bf16[1584,384]{1,0:T(8,128)(2,1)}, f32[1584,384]{1,0:T(8,128)}, f32[3,48,384]{2,1,0:T(8,128)}, f32[16,1536]{1,0:T(8,128)}, f32[8,128]{1,0:T(8,128)}) custom-call(bf16[1584,384]{1,0:T(8,128)(2,1)} %x_h.1, s32[16,198]{1,0:T(8,128)} %reshape.51.keep_v, bf16[1584,384]{1,0:T(8,128)(2,1)} %cot_h.1, f32[3,24,192]{2,1,0:T(8,128)} %refs_5_.1, ...), custom_call_target="tpu_custom_call" | custom-call | tf_op jit(solution)/shard_map/pallas_call | solution.py:749
  132.5 5.5 %shard_map.389 = (bf16[1584,384]{1,0:T(8,128)(2,1)}, f32[1584,384]{1,0:T(8,128)}, f32[3,24,192]{2,1,0:T(8,128)}, f32[3,24,192]{2,1,0:T(8,128)}, f32[3,24,192]{2,...) custom-call(f32[3,48,384]{2,1,0:T(8,128)} %get-tuple-element.53.refs, ...), custom_call_target="tpu_custom_call" | custom-call | tf_op jit(solution)/shard_map/pallas_call | solution.py:773

commit v3 on v2

v3 whole, which is shorter than its diff:
```python
import functools

import jax
import jax.numpy as jnp
from jax import lax
from jax.experimental import pallas as pl
from jax.experimental.pallas import tpu as pltpu
from jax.sharding import PartitionSpec as P

HEAD_DIM = 64
PATCHES = 196
STEP = 5

norm_eps = 1e-06
beta_one = 0.9
beta_two = 0.999
adam_eps = 1e-08
matrix_decay = 0.05

F32 = jnp.float32
BF16 = jnp.bfloat16
MESH = pl.DeviceIdType.MESH
SEQ = PATCHES + 2
PAD = 208
NEG = -1000000000.0
SCALE = HEAD_DIM**-0.5
G_QKV, G_MID, G_FF, G_BACK, G_LAST = 8, 4, 8, 4, 4
U_ATT, U_ATB = 4, 2


def dot_nn(a, b):
    return lax.dot_general(a, b, (((1,), (0,)), ((), ())), preferred_element_type=F32)


def dot_nt(a, b):
    return lax.dot_general(a, b, (((1,), (1,)), ((), ())), preferred_element_type=F32)


def dot_tn(a, b):
    return lax.dot_general(a, b, (((0,), (0,)), ((), ())), preferred_element_type=F32)


def norm_parts(v):
    mean = jnp.mean(v, axis=-1, keepdims=True)
    centred = v - mean
    var = jnp.mean(centred * centred, axis=-1, keepdims=True)
    rstd = lax.rsqrt(var + norm_eps)
    return centred * rstd, rstd


def norm_back(grad, xhat, rstd, gain):
    u = grad * gain
    return (
        u
        - jnp.mean(u, axis=-1, keepdims=True)
        - xhat * jnp.mean(u * xhat, axis=-1, keepdims=True)
    ) * rstd


def gelu_parts(u):
    cdf = 0.5 + 0.5 * lax.erf(0.7071067811865476 * u)
    return u * cdf, cdf + u * (0.3989422804014327 * jnp.exp(-0.5 * u * u))


def adam(master, first, second, grad, rate, decay):
    first = beta_one * first + (1.0 - beta_one) * grad
    second = beta_two * second + (1.0 - beta_two) * grad * grad
    first_hat = first / (1.0 - beta_one**STEP)
    second_hat = second / (1.0 - beta_two**STEP)
    master = master - rate * (first_hat / (jnp.sqrt(second_hat) + adam_eps) + decay * master)
    return first, second, master


def piece_parts(piece, tt, hw, width):
    if piece == 0:
        return [(b, 0, 128, 384 * tt + 128 * b) for b in range(3)]
    if piece == 1:
        at, rest = 768, hw - 128
        proj = 1152 + hw * tt
        return [
            (0, 0, rest, at + rest * tt),
            (0, rest, rest, at + 128 + rest * tt),
            (1, 0, rest, at + 256 + rest * tt),
            (1, rest, rest, proj),
            (2, 0, 128, proj + rest),
        ]
    return [(0, 0, width, width * tt), (1, 0, width, 2 * width + width * tt)]


def kernel(
    nl,
    np_,
    x_h,
    keep_v,
    cot_h,
    qm,
    pm,
    am,
    cm,
    nm,
    bm,
    out_h,
    gin_h,
    fin_a,
    fin_m,
    vec_o,
    kept_o,
    wba,
    wbm,
    w_qkv,
    w_proj,
    w_ff,
    grd,
    sib_a,
    sib_m,
    rpl_a,
    rpl_m,
    lsn_a,
    lsn_m,
    rln_a,
    rln_m,
    pk_a,
    pk_m,
    bias2,
    cntl,
    cntp,
    vec,
    vsib,
    vpl,
    vln,
    stage,
    mid,
    acc_o,
    acc_d,
    probs,
    mcol,
    mkt,
    xpad,
    back,
    n1,
    qkv,
    att,
    n2,
    gbr,
    gatt,
    opad,
    act,
    gp,
    dqkv,
    dma_sem,
    ag_ls,
    ag_lr,
    ag_ps,
    ag_pr,
    ag_ss,
    ag_sr,
    rs_ss,
    rs_sr,
    rs_ps,
    rs_pr,
    rs_ls,
    rs_lr,
    cn_s,
    cn_r,
    cm_s,
    cm_r,
    vs_s,
    vs_r,
):
    rows, dim = x_h.shape
    images = rows // SEQ
    r = qm.shape[1]
    hw = qm.shape[2]
    width = wbm.shape[5]
    chunks = wbm.shape[0]
    chunk = 2 * width
    heads = dim // HEAD_DIM
    t = lax.axis_index("tp")
    d = lax.axis_index("dp")
    l = d // np_
    p = d - l * np_
    o = 1 - t
    first_half = t == 0

    def at(ll, pp):
        return {"dp": ll * np_ + pp}

    def line_peer(k):
        return lax.rem(l + k, nl)

    def line_from(k):
        return lax.rem(l + nl - k, nl)

    def plane_peer(k):
        return lax.rem(p + k, np_)

    def plane_from(k):
        return lax.rem(p + np_ - k, np_)

    x_in = pltpu.make_async_copy(x_h, dqkv.at[0:rows, 0:dim], dma_sem.at[0])
    c_in = pltpu.make_async_copy(cot_h, dqkv.at[0:rows, dim : 2 * dim], dma_sem.at[1])
    x_in.start()
    c_in.start()

    barrier = pltpu.get_barrier_semaphore()
    for k in range(1, nl):
        pl.semaphore_signal(barrier, inc=1, device_id=at(line_peer(k), p), device_id_type=MESH)
    for k in range(1, np_):
        pl.semaphore_signal(barrier, inc=1, device_id=at(l, plane_peer(k)), device_id_type=MESH)
    pl.semaphore_signal(barrier, inc=1, device_id={"tp": o}, device_id_type=MESH)

    def w_buf(pc):
        return wba.at[pc] if pc < 2 else wbm.at[pc - 2]

    def of(a_ref, m_ref, pc):
        return a_ref.at[pc] if pc < 2 else m_ref.at[pc - 2]

    def stacked(pc, blocks):
        pk = pk_a if pc < 2 else pk_m
        have, need = r * len(blocks), pk.shape[0]
        if r % 8 == 0:
            pad = [jnp.zeros((need - have, pk.shape[1]), F32)] if need > have else []
            return jnp.concatenate(list(blocks) + pad, axis=0)
        if need > have:
            pk[...] = jnp.zeros_like(pk)
        for b, block in enumerate(blocks):
            pk[b * r : (b + 1) * r, :] = block
        return pk[...]

    def either(a, b):
        return jnp.where(first_half, a, b)

    rest = hw - 128
    q3 = [qm[c] for c in range(3)]
    big = [either(q[:, 0:128], q[:, rest:]) for q in q3]
    small = [either(q[:, 128:], q[:, 0:rest]) for q in q3]
    wba[0, t, p, l] = stacked(0, big).astype(BF16)
    proj_own = pm[...]
    wba[1, t, p, l] = stacked(
        1,
        [
            jnp.concatenate([small[0], small[1]], axis=1),
            jnp.concatenate([small[2], proj_own[:, 0:rest]], axis=1),
            proj_own[:, rest:],
        ],
    ).astype(BF16)
    for j in range(chunks):
        cols = slice(j * width, (j + 1) * width)
        wbm[j, t, p, l] = stacked(2 + j, [am[:, cols], cm[:, cols]]).astype(BF16)
    bias2[t] = jnp.broadcast_to(bm[...], bias2.shape[1:])
    keep_all = keep_v[...].astype(F32)
    count = jnp.sum(jnp.sum(keep_all, axis=1, keepdims=True), axis=0, keepdims=True)
    cntl[l] = jnp.broadcast_to(count, cntl.shape[1:])

    pl.semaphore_wait(barrier, nl - 1 + np_ - 1 + 1)

    def remote(src, dst, ssem, rsem, device):
        return pltpu.make_async_remote_copy(
            src_ref=src, dst_ref=dst, send_sem=ssem, recv_sem=rsem, device_id=device, device_id_type=MESH
        )

    def got(dst, rsem):
        return remote(dst, dst, dma_sem.at[2], rsem, {"tp": o})

    sends = {pc: [] for pc in range(2 + chunks)}

    def send(pc, src, dst, ssem, rsem, device):
        cp = remote(src, dst, ssem, rsem, device)
        cp.start()
        sends[pc].append(cp)

    def to_plane(pc, ll, kl):
        here = w_buf(pc).at[t, p, ll]
        for k in range(1, np_):
            send(pc, here, here, ag_ps.at[pc, kl, k], ag_pr.at[pc, kl, k], at(l, plane_peer(k)))

    def start_piece(pc):
        here = w_buf(pc).at[t, p, l]
        for k in range(1, nl):
            send(pc, here, here, ag_ls.at[pc, k], ag_lr.at[pc, k], at(line_peer(k), p))
        to_plane(pc, l, 0)

    def line_done(pc):
        for k in range(1, nl):
            ll = line_from(k)
            got(w_buf(pc).at[t, p, ll], ag_lr.at[pc, k]).wait_recv()
            to_plane(pc, ll, k)
        here = w_buf(pc).at[t, p]
        send(pc, here, here, ag_ss.at[pc, 0], ag_sr.at[pc, 0], {"tp": o})

    def plane_done(pc):
        for k in range(1, np_):
            pp = plane_from(k)
            for kl in range(nl):
                got(w_buf(pc).at[t, pp, line_from(kl) if kl else l], ag_pr.at[pc, kl, k]).wait_recv()
            here = w_buf(pc).at[t, pp]
            send(pc, here, here, ag_ss.at[pc, k], ag_sr.at[pc, k], {"tp": o})

    def sibling_done(pc):
        for k in range(np_):
            got(w_buf(pc).at[o, plane_from(k) if k else p], ag_sr.at[pc, k]).wait_recv()

    def assemble(pc):
        for tt in range(2):
            for ll in range(nl):
                for pp in range(np_):
                    slot = w_buf(pc)[tt, pp, ll].astype(F32)
                    row = (ll * np_ + pp) * r
                    for b, lane_at, cols, col in piece_parts(pc, tt, hw, width):
                        grd[row : row + r, col : col + cols] = slot[b * r : (b + 1) * r, lane_at : lane_at + cols]
        if pc == 0:
            w_qkv[:, 0:768] = grd[:, 0:768].astype(BF16)
        elif pc == 1:
            w_qkv[:, 768:1152] = grd[:, 768:1152].astype(BF16)
            w_proj[...] = grd[:, 1152:1536].astype(BF16)
        else:
            w_ff[pc - 2] = grd[:, 0 : 2 * chunk].astype(BF16)

    start_piece(0)
    send(0, bias2.at[t], bias2.at[t], cm_s.at[0], cm_r.at[0], {"tp": o})
    for k in range(1, nl):
        send(0, cntl.at[l], cntl.at[l], cn_s.at[k], cn_r.at[k], at(line_peer(k), p))

    def cast_in(col):
        def step(c, carry):
            at_row = pl.ds(pl.multiple_of(c * 16, 16), 16)
            stage[at_row, :] = dqkv[at_row, col : col + dim].astype(F32)
            return carry

        lax.fori_loop(0, rows // 16, step, 0)

    stage[rows:, :] = jnp.zeros((stage.shape[0] - rows, dim), F32)
    own_keep = keep_v[pl.ds(pl.multiple_of(t * images, images), images), :].astype(F32)
    mkt[...] = jnp.zeros_like(mkt)
    mkt[0:images, 0:SEQ] = own_keep
    keep_t = mkt[...].T
    for i in range(images):
        mcol[i] = jnp.broadcast_to(keep_t[0:PAD, i : i + 1], (PAD, 128))
    inside = lax.broadcasted_iota(jnp.int32, (PAD, dim), 0) < SEQ
    x_in.wait()
    cast_in(0)
    gain1, shift1 = nm[0:1, :], nm[1:2, :]

    def norm_in(i):
        v = jnp.where(inside, stage[i * SEQ : i * SEQ + PAD, :], 0.0)
        xpad[i * PAD : (i + 1) * PAD, :] = v.astype(BF16)
        xhat, _ = norm_parts(v)
        n1[i * PAD : (i + 1) * PAD, :] = (xhat * gain1 + shift1).astype(BF16)

    for i in range(images // 4):
        norm_in(i)
    line_done(0)
    start_piece(1)
    for k in range(1, nl):
        got(cntl.at[line_from(k)], cn_r.at[k]).wait_recv()
    cntp[p] = functools.reduce(lambda a, b: a + b, [cntl[ll] for ll in range(nl)])
    for k in range(1, np_):
        send(0, cntp.at[p], cntp.at[p], cm_s.at[k], cm_r.at[k], at(l, plane_peer(k)))
    for i in range(images // 4, images):
        norm_in(i)
    plane_done(0)
    line_done(1)
    for j in range(chunks):
        start_piece(2 + j)
    sibling_done(0)
    got(bias2.at[o], cm_r.at[0]).wait_recv()
    assemble(0)

    def image_rows(i, many=1):
        return pl.ds(pl.multiple_of(i * (many * PAD), 16), many * PAD)

    def over_images(step, many=1, unroll=1):
        lax.fori_loop(0, images // many, lambda i, carry: step(i) or carry, 0, unroll=unroll)

    order = (0, 2, 1)
    both = [bias2[0, 0:1, :], bias2[1, 0:1, :]]
    q_bias = jnp.concatenate([b[:, 0:hw] for b in both], axis=1)
    v_bias = jnp.concatenate([b[:, hw : 2 * hw] for b in both], axis=1)
    h_bias = [
        jnp.concatenate([b[:, 2 * hw + j * width : 2 * hw + (j + 1) * width] for b in both], axis=1)
        for j in range(chunks)
    ]

    def pair_bias(pos):
        cols = slice(128 * order[pos], 128 * order[pos] + 128)
        return jnp.concatenate([q_bias[:, cols], jnp.zeros((1, 128), F32), v_bias[:, cols]], axis=1)

    def qkv_rows(group):
        cols = slice(384 * group[0], 384 * group[-1] + 384)
        bias = jnp.concatenate([pair_bias(pos) for pos in group], axis=1)

        def step(i):
            here = image_rows(i, G_QKV)
            qkv[here, cols] = (dot_nn(n1[here, :], w_qkv[:, cols]) + bias).astype(BF16)

        over_images(step, G_QKV)

    lane = lax.broadcasted_iota(jnp.int32, (1, 128), 1)
    head_mask = [(lane < HEAD_DIM).astype(F32).astype(BF16), (lane >= HEAD_DIM).astype(F32).astype(BF16)]
    head_scale = [(SCALE * mask.astype(F32)).astype(BF16) for mask in head_mask]

    def attend(group):
        def step(i):
            here = image_rows(i)
            m = mcol[i]
            m = jnp.concatenate([m, m], axis=1)[:, 0:PAD] > 0.0
            for pos in group:
                c = order[pos]
                qp, kp, vp = (qkv[here, 384 * pos + 128 * b : 384 * pos + 128 * b + 128] for b in range(3))
                total = None
                for h in range(2):
                    s = jnp.where(m, dot_nt(kp * head_scale[h], qp), NEG)
                    e = jnp.exp(s - jnp.max(s, axis=0, keepdims=True))
                    pr = e * (1.0 / jnp.sum(e, axis=0, keepdims=True))
                    probs[i * heads + 2 * pos + h] = pr
                    term = dot_tn(pr.astype(BF16), vp * head_mask[h])
                    total = term if total is None else total + term
                att[here, c * 128 : (c + 1) * 128] = total.astype(BF16)

        over_images(step, unroll=U_ATT)

    qkv_rows((0, 1))
    plane_done(1)
    line_done(2)
    attend((0, 1))
    sibling_done(1)
    for j in range(1, chunks):
        line_done(2 + j)
    assemble(1)
    qkv_rows((2,))
    plane_done(2)

    c_in.wait()
    cast_in(dim)
    for i in range(images):
        v = jnp.where(inside, stage[i * SEQ : i * SEQ + PAD, :], 0.0)
        m = mcol[i]
        back[i * PAD : (i + 1) * PAD, :] = (v * jnp.concatenate([m] * (dim // 128), axis=1)).astype(BF16)
    attend((2,))
    for j in range(1, chunks):
        plane_done(2 + j)
    for k in range(1, np_):
        got(cntp.at[plane_from(k)], cm_r.at[k]).wait_recv()
    kept = functools.reduce(lambda a, b: a + b, [cntp[pp] for pp in range(np_)])
    grad_scale = (rows * 2.0 * nl * np_) / kept[0:1, 0:1]

    vec[...] = jnp.zeros_like(vec)
    bias4, gain2, shift2, bias5 = nm[4:5, :], nm[2:3, :], nm[3:4, :], nm[5:6, :]

    def mid_step(i):
        here = image_rows(i, G_MID)
        m = xpad[here, :].astype(F32) + (dot_nt(att[here, :], w_proj[...]) + bias4)
        mid[here, :] = m
        xhat, _ = norm_parts(m)
        n2[here, :] = (xhat * gain2 + shift2).astype(BF16)

    over_images(mid_step, G_MID)

    def pack(pc):
        for cp in sends[pc]:
            cp.wait_send()
        for tt in range(2):
            parts = piece_parts(pc, tt, hw, width)
            for ll in range(nl):
                for pp in range(np_):
                    row = (ll * np_ + pp) * r
                    blocks = []
                    for b in range(parts[-1][0] + 1):
                        own = [grd[row : row + r, col : col + cols] for bb, _, cols, col in parts if bb == b]
                        blocks.append(jnp.concatenate(own, axis=1) if len(own) > 1 else own[0])
                    w_buf(pc)[tt, pp, ll] = stacked(pc, blocks).astype(BF16)

    late = []

    def send_late(src, dst, ssem, rsem, device):
        cp = remote(src, dst, ssem, rsem, device)
        cp.start()
        late.append(cp)

    def send_sibling(pc):
        send_late(w_buf(pc).at[o], of(sib_a, sib_m, pc), rs_ss.at[pc], rs_sr.at[pc], {"tp": o})

    def send_plane(pc):
        sib, rpl = of(sib_a, sib_m, pc), of(rpl_a, rpl_m, pc)
        got(sib, rs_sr.at[pc]).wait_recv()
        for pp in range(np_):
            for ll in range(nl):
                sib[pp, ll] = (sib[pp, ll].astype(F32) + w_buf(pc)[t, pp, ll].astype(F32)).astype(BF16)
        for k in range(1, np_):
            send_late(sib.at[plane_peer(k)], rpl.at[p], rs_ps.at[pc, k], rs_pr.at[pc, k], at(l, plane_peer(k)))
        rpl[p] = sib[p]

    def send_line(pc):
        rpl, lsn, rln = of(rpl_a, rpl_m, pc), of(lsn_a, lsn_m, pc), of(rln_a, rln_m, pc)
        for k in range(1, np_):
            got(rpl.at[plane_from(k)], rs_pr.at[pc, k]).wait_recv()
        for ll in range(nl):
            lsn[ll] = functools.reduce(
                lambda a, b: a + b, [rpl[pp, ll].astype(F32) for pp in range(np_)]
            ).astype(BF16)
        for k in range(1, nl):
            send_late(lsn.at[line_peer(k)], rln.at[l], rs_ls.at[pc, k], rs_lr.at[pc, k], at(line_peer(k), p))
        rln[l] = lsn[l]

    def sum_line(pc):
        rln, fin = of(rln_a, rln_m, pc), of(fin_a, fin_m, pc)
        for k in range(1, nl):
            got(rln.at[line_from(k)], rs_lr.at[pc, k]).wait_recv()
        fin[...] = functools.reduce(lambda a, b: a + b, [rln[ll].astype(F32) for ll in range(nl)])

    def ff_chunk(j):
        def step(i):
            here = image_rows(i, G_FF)
            b = back[here, :]
            w1, w2 = w_ff[j, :, 0:chunk], w_ff[j, :, chunk : 2 * chunk]
            pre = dot_nn(n2[here, :], w1) + h_bias[j]
            ga = dot_nn(b, w2)
            value, slope = gelu_parts(pre)
            value = value.astype(BF16)
            gpre = (ga * slope).astype(BF16)
            act[here, :] = value
            gp[here, :] = gpre
            vec[8 + j : 9 + j, :] += jnp.sum(gpre.astype(F32), axis=0, keepdims=True)
            term_o = dot_nt(value, w2)
            term_d = dot_nt(gpre, w1)
            if j == 0:
                acc_o[here, :] = term_o
                acc_d[here, :] = term_d
            else:
                acc_o[here, :] += term_o
                acc_d[here, :] += term_d

        over_images(step, G_FF)
        grd[:, 0:chunk] = dot_tn(n2[...], gp[...])
        grd[:, chunk : 2 * chunk] = dot_tn(back[...], act[...])

    for j in range(chunks):
        sibling_done(2 + j)
        assemble(2 + j)
        ff_chunk(j)
        pack(2 + j)
        send_sibling(2 + j)
        if j > 0:
            send_line(1 + j)
        send_plane(2 + j)

    def back_step(i):
        here = image_rows(i, G_BACK)
        m = mid[here, :]
        opad[here, :] = (m + (acc_o[here, :] + bias5)).astype(BF16)
        xhat, rstd = norm_parts(m)
        dn = acc_d[here, :]
        bfl = back[here, :].astype(F32)
        gm = bfl + norm_back(dn, xhat, rstd, gain2)
        mid[here, :] = gm
        g16 = gm.astype(BF16)
        gbr[here, :] = g16
        gatt[here, :] = dot_nn(g16, w_proj[...]).astype(BF16)
        vec[2:3, 0:dim] += jnp.sum(dn * xhat, axis=0, keepdims=True)
        vec[3:4, 0:dim] += jnp.sum(dn, axis=0, keepdims=True)
        vec[4:5, 0:dim] += jnp.sum(g16.astype(F32), axis=0, keepdims=True)
        vec[5:6, 0:dim] += jnp.sum(bfl, axis=0, keepdims=True)

    over_images(back_step, G_BACK)

    def attend_back(group):
        def step(i):
            here = image_rows(i)
            for pos in group:
                c = order[pos]
                qp, kp, vp = (qkv[here, 384 * pos + 128 * b : 384 * pos + 128 * b + 128] for b in range(3))
                da = gatt[here, c * 128 : (c + 1) * 128]
                dq = dk = dv = 0.0
                for h in range(2):
                    hm = head_mask[h]
                    pr = probs[i * heads + 2 * pos + h]
                    dp = dot_nt(vp * hm, da)
                    inner = jnp.sum(pr * dp, axis=0, keepdims=True)
                    ds = (pr * (dp - inner)).astype(BF16)
                    dv = dv + dot_nn(pr.astype(BF16), da * hm)
                    dk = dk + dot_nn(ds, qp * head_scale[h])
                    dq = dq + dot_tn(ds, kp * head_scale[h])
                dq = dq.astype(BF16)
                dv = dv.astype(BF16)
                dqkv[here, 384 * pos : 384 * pos + 128] = dq
                dqkv[here, 384 * pos + 128 : 384 * pos + 256] = dk.astype(BF16)
                dqkv[here, 384 * pos + 256 : 384 * pos + 384] = dv
                vec[6:7, c * 128 : (c + 1) * 128] += jnp.sum(dq.astype(F32), axis=0, keepdims=True)
                vec[7:8, c * 128 : (c + 1) * 128] += jnp.sum(dv.astype(F32), axis=0, keepdims=True)

        over_images(step, unroll=U_ATB)

    attend_back((0, 1))
    send_line(1 + chunks)
    for pos in range(2):
        cols = slice(384 * pos, 384 * pos + 384)
        grd[:, cols] = dot_tn(n1[...], dqkv[:, cols])
    pack(0)
    send_sibling(0)
    grd[:, 1152:1536] = dot_tn(gbr[...], att[...])
    send_plane(0)
    attend_back((2,))
    grd[:, 768:1152] = dot_tn(n1[...], dqkv[:, 768:1152])
    pack(1)
    send_sibling(1)
    send_line(0)
    send_plane(1)

    def last_step(i):
        here = image_rows(i, G_LAST)
        dn = dot_nt(dqkv[here, :], w_qkv[...])
        xhat, rstd = norm_parts(xpad[here, :].astype(F32))
        mid[here, :] = (mid[here, :] + norm_back(dn, xhat, rstd, gain1)) * grad_scale
        vec[0:1, 0:dim] += jnp.sum(dn * xhat, axis=0, keepdims=True)
        vec[1:2, 0:dim] += jnp.sum(dn, axis=0, keepdims=True)

    over_images(last_step, G_LAST)
    send_late(vec, vsib, vs_s.at[0], vs_r.at[0], {"tp": o})

    for i in range(images):
        stage[i * SEQ : (i + 1) * SEQ, :] = opad[i * PAD : i * PAD + SEQ, :].astype(F32)

    def cast_out(c, carry):
        at_row = pl.ds(pl.multiple_of(c * 16, 16), 16)
        n2[at_row, :] = stage[at_row, :].astype(BF16)
        return carry

    lax.fori_loop(0, rows // 16, cast_out, 0)
    out_cp = pltpu.make_async_copy(n2.at[0:rows, :], out_h, dma_sem.at[0])
    out_cp.start()
    got(vsib, vs_r.at[0]).wait_recv()
    vpl[p] = vec[...] + vsib[...]
    for k in range(1, np_):
        send_late(vpl.at[p], vpl.at[p], vs_s.at[k], vs_r.at[k], at(l, plane_peer(k)))
    for i in range(images):
        stage[i * SEQ : (i + 1) * SEQ, :] = mid[i * PAD : i * PAD + SEQ, :]
    gin_cp = pltpu.make_async_copy(stage.at[0:rows, :], gin_h, dma_sem.at[1])
    gin_cp.start()
    send_line(1)
    for k in range(1, np_):
        got(vpl.at[plane_from(k)], vs_r.at[k]).wait_recv()
    vln[l] = functools.reduce(lambda a, b: a + b, [vpl[pp] for pp in range(np_)])
    for k in range(1, nl):
        send_late(vln.at[l], vln.at[l], vs_s.at[np_ + k], vs_r.at[np_ + k], at(line_peer(k), p))
    kept_o[...] = kept
    for pc in range(2, 2 + chunks):
        sum_line(pc)
    sum_line(0)
    sum_line(1)
    for k in range(1, nl):
        got(vln.at[line_from(k)], vs_r.at[np_ + k]).wait_recv()
    vec_o[...] = functools.reduce(lambda a, b: a + b, [vln[ll] for ll in range(nl)])
    out_cp.wait()
    gin_cp.wait()
    for cp in late:
        cp.wait_send()


def update_kernel(scale_rows, *refs):
    fin_a, fin_m, vec, kept, out_in, gin_in = refs[:6]
    states = [refs[6 + 3 * k : 9 + 3 * k] for k in range(6)]
    out_h, gin_h = refs[24:26]
    q_o, p_o, a_o, c_o = (refs[26 + 4 * k : 30 + 4 * k] for k in range(4))
    n_o, b_o = refs[42:45], refs[45:48]
    out_v, gin_v, sems_in, sems_out = refs[48:]
    parts = 3
    size = out_in.shape[0] // parts
    loads, stores = [], []
    for k in range(parts):
        here = pl.ds(k * size, size)
        for j, (src, via, dst) in enumerate(((out_in, out_v, out_h), (gin_in, gin_v, gin_h))):
            loads.append(pltpu.make_async_copy(src.at[here, :], via.at[here, :], sems_in.at[j, k]))
            stores.append(pltpu.make_async_copy(via.at[here, :], dst.at[here, :], sems_out.at[j, k]))
    for cp in loads:
        cp.start()
    for load, store in zip(loads, stores):
        load.wait()
        store.start()
    qkv, proj, fc1, fc2, norm, bias = states
    r, hw = proj[0].shape
    rest = hw - 128
    chunks, _, width = fin_m.shape
    own = lax.axis_index("tp") == 0
    grad_scale = scale_rows / kept[0:1, 0:1]

    def update(grad, state, outs, rate, decay, c=None):
        pick = (lambda ref: ref[...]) if c is None else (lambda ref: ref[c])
        master, first, second = (pick(ref) for ref in state)
        first, second, master = adam(master, first, second, grad * grad_scale, rate, decay)
        for ref, value in zip(outs, (first, second, master, master)):
            if c is None:
                ref[...] = value.astype(ref.dtype)
            else:
                ref[c] = value.astype(ref.dtype)

    big, small = fin_a[0], fin_a[1]
    pieces = (small[0:r, 0:rest], small[0:r, rest:], small[r : 2 * r, 0:rest])
    for c in range(3):
        first, second = big[c * r : (c + 1) * r, :], pieces[c]
        grad = jnp.where(
            own, jnp.concatenate([first, second], axis=1), jnp.concatenate([second, first], axis=1)
        )
        update(grad, qkv, q_o, 0.08, matrix_decay, c)
    update(
        jnp.concatenate([small[r : 2 * r, rest:], small[2 * r : 3 * r, :]], axis=1), proj, p_o, 0.8, matrix_decay
    )
    update(jnp.concatenate([fin_m[j, 0:r, :] for j in range(chunks)], axis=1), fc1, a_o, 0.08, matrix_decay)
    update(jnp.concatenate([fin_m[j, r : 2 * r, :] for j in range(chunks)], axis=1), fc2, c_o, 0.04, matrix_decay)
    update(vec[0:6, 0 : norm[0].shape[1]], norm, n_o, 0.5, 0.0)

    def pick(row, cols):
        return jnp.where(own, vec[row : row + 1, 0:cols], vec[row : row + 1, cols : 2 * cols])

    bias_parts = [pick(6, hw), pick(7, hw)] + [pick(8 + j, width) for j in range(chunks)]
    update(jnp.concatenate(bias_parts, axis=1), bias, b_o, 0.5, 0.0)
    for store in stores:
        store.wait()


def body(
    inputs, keep_mask, cotangent,
    qkv_master, qkv_first, qkv_second,
    proj_master, proj_first, proj_second,
    fc1_master, fc1_first, fc1_second,
    fc2_master, fc2_first, fc2_second,
    norm_master, norm_first, norm_second,
    bias_master, bias_first, bias_second,
):
    n = lax.axis_size("dp")
    nl = 4 if n % 4 == 0 else n
    np_ = n // nl
    rows, dim = inputs.shape
    images = rows // SEQ
    padded = images * PAD
    r = qkv_master.shape[1]
    hw = qkv_master.shape[2]
    fw = fc1_master.shape[1]
    width = 256
    chunks = fw // width
    chunk = 2 * width
    slot_a = -(-3 * r // 16) * 16
    slot_m = -(-2 * r // 16) * 16
    keep = keep_mask.reshape(2 * images, SEQ)
    vm = pl.BlockSpec(memory_space=pltpu.VMEM)
    hbm = pl.BlockSpec(memory_space=pl.ANY)

    def like(a, dtype=None):
        return jax.ShapeDtypeStruct(a.shape, dtype or a.dtype)

    proj_master, proj_first, proj_second = proj_master.T, proj_first.T, proj_second.T
    fc2_master, fc2_first, fc2_second = fc2_master.T, fc2_first.T, fc2_second.T
    large = [like(inputs), like(inputs, F32)]
    sums = [
        jax.ShapeDtypeStruct((2, slot_a, 128), F32),
        jax.ShapeDtypeStruct((chunks, slot_m, width), F32),
        jax.ShapeDtypeStruct((16, chunk), F32),
        jax.ShapeDtypeStruct((8, 128), F32),
    ]
    dma = pltpu.SemaphoreType.DMA
    pieces = 2 + chunks
    scratch = [
        pltpu.VMEM((2, 2, np_, nl, slot_a, 128), BF16),
        pltpu.VMEM((chunks, 2, np_, nl, slot_m, width), BF16),
        pltpu.VMEM((dim, 3 * dim), BF16),
        pltpu.VMEM((dim, dim), BF16),
        pltpu.VMEM((chunks, dim, 2 * chunk), BF16),
        pltpu.VMEM((dim, 4 * dim), F32),
        pltpu.VMEM((2, np_, nl, slot_a, 128), BF16),
        pltpu.VMEM((chunks, np_, nl, slot_m, width), BF16),
        pltpu.VMEM((2, np_, nl, slot_a, 128), BF16),
        pltpu.VMEM((chunks, np_, nl, slot_m, width), BF16),
        pltpu.VMEM((2, nl, slot_a, 128), BF16),
        pltpu.VMEM((chunks, nl, slot_m, width), BF16),
        pltpu.VMEM((2, nl, slot_a, 128), BF16),
        pltpu.VMEM((chunks, nl, slot_m, width), BF16),
        pltpu.VMEM((slot_a, 128), F32),
        pltpu.VMEM((slot_m, width), F32),
        pltpu.VMEM((2, 8, bias_master.shape[1]), F32),
        pltpu.VMEM((nl, 8, 128), F32),
        pltpu.VMEM((np_, 8, 128), F32),
        pltpu.VMEM((16, chunk), F32),
        pltpu.VMEM((16, chunk), F32),
        pltpu.VMEM((np_, 16, chunk), F32),
        pltpu.VMEM((nl, 16, chunk), F32),
        pltpu.VMEM((-(-(rows - SEQ + PAD) // 16) * 16, dim), F32),
        pltpu.VMEM((padded, dim), F32),
        pltpu.VMEM((padded, dim), F32),
        pltpu.VMEM((padded, dim), F32),
        pltpu.VMEM((images * (dim // HEAD_DIM), PAD, PAD), F32),
        pltpu.VMEM((images, PAD, 128), F32),
        pltpu.VMEM((128, 256), F32),
        pltpu.VMEM((padded, dim), BF16),
        pltpu.VMEM((padded, dim), BF16),
        pltpu.VMEM((padded, dim), BF16),
        pltpu.VMEM((padded, 3 * dim), BF16),
        pltpu.VMEM((padded, dim), BF16),
        pltpu.VMEM((padded, dim), BF16),
        pltpu.VMEM((padded, dim), BF16),
        pltpu.VMEM((padded, dim), BF16),
        pltpu.VMEM((padded, dim), BF16),
        pltpu.VMEM((padded, chunk), BF16),
        pltpu.VMEM((padded, chunk), BF16),
        pltpu.VMEM((padded, 3 * dim), BF16),
        dma((3,)),
        dma((pieces, nl)),
        dma((pieces, nl)),
        dma((pieces, nl, np_)),
        dma((pieces, nl, np_)),
        dma((pieces, np_)),
        dma((pieces, np_)),
        dma((pieces,)),
        dma((pieces,)),
        dma((pieces, np_)),
        dma((pieces, np_)),
        dma((pieces, nl)),
        dma((pieces, nl)),
        dma((nl,)),
        dma((nl,)),
        dma((np_,)),
        dma((np_,)),
        dma((np_ + nl,)),
        dma((np_ + nl,)),
    ]
    out, gin, fin_a, fin_m, vec, kept = pl.pallas_call(
        functools.partial(kernel, nl, np_),
        out_shape=large + sums,
        in_specs=[hbm, vm, hbm] + [vm] * 6,
        out_specs=[hbm, hbm] + [vm] * 4,
        scratch_shapes=scratch,
        compiler_params=pltpu.CompilerParams(
            collective_id=0, has_side_effects=True, vmem_limit_bytes=64 * 1024 * 1024
        ),
    )(inputs, keep, cotangent, qkv_master, proj_master, fc1_master, fc2_master, norm_master, bias_master)
    states = [
        qkv_master, qkv_first, qkv_second,
        proj_master, proj_first, proj_second,
        fc1_master, fc1_first, fc1_second,
        fc2_master, fc2_first, fc2_second,
        norm_master, norm_first, norm_second,
        bias_master, bias_first, bias_second,
    ]
    outs = list(large)
    for a in (qkv_master, proj_master, fc1_master, fc2_master):
        outs += [like(a), like(a), like(a), like(a, BF16)]
    for a in (norm_master, bias_master):
        outs += [like(a)] * 3
    res = list(
        pl.pallas_call(
            functools.partial(update_kernel, rows * 2.0 * n),
            out_shape=outs,
            in_specs=[vm] * 4 + [hbm] * 2 + [vm] * 18,
            out_specs=[hbm] * 2 + [vm] * 22,
            scratch_shapes=[pltpu.VMEM((rows, dim), BF16), pltpu.VMEM((rows, dim), F32), dma((2, 3)), dma((2, 3))],
            compiler_params=pltpu.CompilerParams(vmem_limit_bytes=64 * 1024 * 1024),
        )(fin_a, fin_m, vec, kept, out, gin, *states)
    )
    for k in (6, 7, 8, 9, 14, 15, 16, 17):
        res[k] = res[k].T
    return tuple(res)


def solution(mesh):
    mats = [P(None, "dp", "tp"), P("tp", "dp"), P("dp", "tp"), P("tp", "dp")]
    in_specs = [P(("dp", "tp"), None), P("dp"), P(("dp", "tp"), None)]
    out_specs = [P(("dp", "tp"), None), P(("dp", "tp"), None)]
    for m in mats:
        in_specs += [m] * 3
        out_specs += [m] * 4
    in_specs += [P()] * 3 + [P("tp", None)] * 3
    out_specs += [P()] * 3 + [P("tp", None)] * 3
    return jax.shard_map(
        body, mesh=mesh, in_specs=tuple(in_specs), out_specs=tuple(out_specs), check_vma=False
    )
```

time: 138 us -> 99.7 us (0.72)
  Pallas kernels: 136 us -> 97.1 us
    pallas_call x1, Pallas kernels: 130 us -> 91.6 us  [body(): pl.pallas_call(functools.partial(kernel, nl, np_), out_shape=large + sums...]
where the time goes in v3:
time: 99.7 us; the launch traced here: 99.4 us
  Pallas kernels  97.1 us (97%)
  local copies, waits for them, and re-layouts  1.42 us (1%)
    pallas_call x1, Pallas kernels, body(): pl.pallas_call(functools.partial(kernel, nl, np_), out_shape=large + sums...  91.6 us
    pallas_call x1, Pallas kernels, body(): pl.pallas_call(functools.partial(update_kernel, rows * 2.0 * n), out_shap...  5.49 us

profile of v3, /device:TPU:0, one launch (start us, length us, event | category | flops | bytes accessed | tf_op | source)
XLA Modules:
  0.0 99.4 jit_solution(8811799360682579795)
XLA Ops:
  0.7 1.4 %reshape.51.keep_v = s32[16,198]{1,0:T(8,128)} reshape(s32[3168]{0:T(1024)} %param.22) | data formatting | bytes 25344 | tf_op jit(solution)/shard_map/reshape | solution.py:743
  2.1 91.6 %shard_map.388 = (bf16[1584,384]{1,0:T(8,128)(2,1)}, f32[1584,384]{1,0:T(8,128)}, f32[2,80,128]{2,1,0:T(8,128)}, f32[3,48,256]{2,1,0:T(8,128)}, f32[16,512]{1,0:T(8,128)}, /*index=5*/f32[8,128]{1,0:T(8,128)}) custom-call(bf16[1584,384]{1,0:T(8,128)(2,1)} %x_h.1, s32[16,198]{1,0:T(8,128)} %reshape.51.keep_v, bf16[1584,384]{1,0:T(8,128)(2,1)} %cot_h.1, ...), custom_call_target="tpu_custom_call" | custom-call | tf_op jit(solution)/shard_map/pallas_call | solution.py:824
  93.7 5.5 %shard_map.389 = (bf16[1584,384]{1,0:T(8,128)(2,1)}, f32[1584,384]{1,0:T(8,128)}, f32[3,24,192]{2,1,0:T(8,128)}, f32[3,24,192]{2,1,0:T(8,128)}, f32[3,24,192]{2,...) custom-call(f32[2,80,128]{2,1,0:T(8,128)} %get-tuple-element.54.refs, ...), custom_call_target="tpu_custom_call" | custom-call | tf_op jit(solution)/shard_map/pallas_call | solution.py:848
